TPU v7x, 32 devices: a whole 2x2x4 slice. The times are simulated.
32 devices in a mesh: dp: 4 (over y, x), mp: 8 (over z, core).
Axes of the slice: x: 2, y: 2, z: 4, core: 2. Of those that a mesh axis runs over, the one named last changes fastest.
Arguments:
- frames: bfloat16 [8, 1664, 1024], P('dp', 'mp'), may hold values from -6 to 6
- lengths: int32 [8], P('dp'), may hold values from 554 to 1664
- mask_flags: int32 [8, 1664], P('dp', 'mp'), may hold values from 0 to 1, as said below
- mask_embed: float32 [1024], replicated, may hold values from -6 to 6
- ffa_gain: float32 [1024], replicated, may hold values from 0.1 to 1.9
- ffa_shift: float32 [1024], replicated, may hold values from -3 to 3
- ffa_w_in: bfloat16 [1024, 4096], P(None, 'mp'), may hold values from -0.1875 to 0.1875
- ffa_b_in: bfloat16 [4096], P('mp'), may hold values from -3 to 3
- ffa_w_out: bfloat16 [4096, 1024], P('mp'), may hold values from -0.1875 to 0.1875
- ffa_b_out: float32 [1024], replicated, may hold values from -3 to 3
- att_gain: float32 [1024], replicated, may hold values from 0.1 to 1.9
- att_shift: float32 [1024], replicated, may hold values from -3 to 3
- att_w_qkv: bfloat16 [3, 1024, 1024], P(None, None, 'mp'), may hold values from -0.1875 to 0.1875
- att_b_qv: float32 [2, 1024], P(None, 'mp'), may hold values from -2.5 to 2.5
- att_w_out: bfloat16 [1024, 1024], P('mp'), may hold values from -1.5 to 1.5
- att_b_out: float32 [1024], replicated, may hold values from -3 to 3
- conv_gain: float32 [1024], replicated, may hold values from 0.1 to 1.9
- conv_shift: float32 [1024], replicated, may hold values from -3 to 3
- conv_w_in: bfloat16 [2, 1024, 1024], P(None, None, 'mp'), may hold values from -0.1875 to 0.1875
- conv_b_in: float32 [2, 1024], P(None, 'mp'), may hold values from -3 to 3
- conv_w_depth: float32 [31, 1024], P(None, 'mp'), may hold values from -1 to 1
- batch_scale: float32 [1024], P('mp'), may hold values from 0.1 to 1.9
- batch_shift: float32 [1024], P('mp'), may hold values from -3 to 3
- running_mean: float32 [1024], P('mp'), may hold values from -3 to 3
- running_var: float32 [1024], P('mp'), may hold values from 0.02 to 0.25
- conv_w_out: bfloat16 [1024, 1024], P('mp'), may hold values from -0.1875 to 0.1875
- conv_b_out: float32 [1024], replicated, may hold values from -3 to 3
- ffb_gain: float32 [1024], replicated, may hold values from 0.1 to 1.9
- ffb_shift: float32 [1024], replicated, may hold values from -3 to 3
- ffb_w_in: bfloat16 [1024, 4096], P(None, 'mp'), may hold values from -0.1875 to 0.1875
- ffb_b_in: bfloat16 [4096], P('mp'), may hold values from -3 to 3
- ffb_w_out: bfloat16 [4096, 1024], P('mp'), may hold values from -0.1875 to 0.1875
- ffb_b_out: float32 [1024], replicated, may hold values from -3 to 3
- final_gain: float32 [1024], replicated, may hold values from 0.1 to 1.9
- final_shift: float32 [1024], replicated, may hold values from -3 to 3
- cotangent: bfloat16 [8, 1664, 1024], P('dp', 'mp'), may hold values from -6 to 6
Outputs:
- layer_out: float32 [8, 1664, 1024], P('dp', 'mp')
- grad_frames: float32 [8, 1664, 1024], P('dp', 'mp')
- grad_mask_embed: float32 [1024], replicated
- grad_ffa_gain: float32 [1024], replicated
- grad_ffa_shift: float32 [1024], replicated
- grad_ffa_w_in: float32 [1024, 4096], P(None, 'mp')
- grad_ffa_b_in: float32 [4096], P('mp')
- grad_ffa_w_out: float32 [4096, 1024], P('mp')
- grad_ffa_b_out: float32 [1024], replicated
- grad_att_gain: float32 [1024], replicated
- grad_att_shift: float32 [1024], replicated
- grad_att_w_qkv: float32 [3, 1024, 1024], P(None, None, 'mp')
- grad_att_b_qv: float32 [2, 1024], P(None, 'mp')
- grad_att_w_out: float32 [1024, 1024], P('mp')
- grad_att_b_out: float32 [1024], replicated
- grad_conv_gain: float32 [1024], replicated
- grad_conv_shift: float32 [1024], replicated
- grad_conv_w_in: float32 [2, 1024, 1024], P(None, None, 'mp')
- grad_conv_b_in: float32 [2, 1024], P(None, 'mp')
- grad_conv_w_depth: float32 [31, 1024], P(None, 'mp')
- grad_batch_scale: float32 [1024], P('mp')
- grad_batch_shift: float32 [1024], P('mp')
- grad_conv_w_out: float32 [1024, 1024], P('mp')
- grad_conv_b_out: float32 [1024], replicated
- grad_ffb_gain: float32 [1024], replicated
- grad_ffb_shift: float32 [1024], replicated
- grad_ffb_w_in: float32 [1024, 4096], P(None, 'mp')
- grad_ffb_b_in: float32 [4096], P('mp')
- grad_ffb_w_out: float32 [4096, 1024], P('mp')
- grad_ffb_b_out: float32 [1024], replicated
- grad_final_gain: float32 [1024], replicated
- grad_final_shift: float32 [1024], replicated
- new_mean: float32 [1024], P('mp')
- new_var: float32 [1024], P('mp')
Inputs may be any that keep to these rules, and one draw needn't show every extreme that they name: `mask_flags`: only frames below the item's length are marked.
All inputs are finite; a program needn't handle non-finite values.
Results may differ from a plain program's by a relative error of at most 0.017.
The roundings to bfloat16 on the way count: a program that leaves them out, or rounds other values in their place, can miss the bound.
Values may be sent and summed in bfloat16 or wider, within the bound.
No kernel may reach another device: no remote copies, remote signals or barrier semaphores. Data moves between devices by JAX's collectives and lax.ppermute only.
A program may use at most 256 MiB of HBM per device.

v0:
```python
import math

import jax
import jax.numpy as jnp
from jax import lax
from jax.sharding import PartitionSpec as P

HEAD = 64


EPS = 1e-05


def norm_forward(values, gain_vec, shift_vec):
    row_mean = jnp.mean(values, axis=-1, keepdims=True)
    centred = values - row_mean
    inv_scale = lax.rsqrt(jnp.mean(centred * centred, axis=-1, keepdims=True) + EPS)
    unit_rows = centred * inv_scale
    return (unit_rows * gain_vec + shift_vec, unit_rows, inv_scale)


def norm_backward(grad_out, unit_rows, inv_scale, gain_vec):
    scaled = grad_out * gain_vec
    grad_in = inv_scale * (
        scaled
        - jnp.mean(scaled, axis=-1, keepdims=True)
        - unit_rows * jnp.mean(scaled * unit_rows, axis=-1, keepdims=True)
    )
    return (grad_in, jnp.sum(grad_out * unit_rows, axis=(0, 1)), jnp.sum(grad_out, axis=(0, 1)))


def swish_slope(values):
    logistic = jax.nn.sigmoid(values)
    return logistic * (1.0 + values * (1.0 - logistic))


def spread_rows(local_rows):
    return lax.all_gather(local_rows, "mp", axis=1, tiled=True)


def collect_rows(partial_rows):
    return lax.psum_scatter(partial_rows, "mp", scatter_dimension=1, tiled=True)


def spread_grads(local_rows):
    return lax.all_gather(local_rows, "mp", axis=1, tiled=True)


def collect_grads(partial_rows):
    return lax.psum_scatter(partial_rows, "mp", scatter_dimension=1, tiled=True)


def ffn_forward(resid, gain_vec, shift_vec, w_in, b_in, w_out, b_out):
    normed, unit_rows, inv_scale = norm_forward(resid, gain_vec, shift_vec)
    act_local = normed.astype(jnp.bfloat16)
    w_in_all, b_in_all, w_out_all = (
        lax.all_gather(w_in, "mp", axis=1, tiled=True),
        lax.all_gather(b_in, "mp", axis=0, tiled=True),
        lax.all_gather(w_out, "mp", axis=0, tiled=True),
    )
    upper_rows = jnp.einsum(
        "ild,dc->ilc", act_local, w_in_all, preferred_element_type=jnp.float32
    ) + b_in_all.astype(jnp.float32)
    swished = jax.nn.silu(upper_rows).astype(jnp.bfloat16)
    partial_out = jnp.einsum("ilc,cd->ild", swished, w_out_all, preferred_element_type=jnp.float32)
    branch = partial_out + b_out
    return (branch, (unit_rows, inv_scale, act_local, upper_rows, swished, w_in_all, w_out_all))


def ffn_backward(grad_resid, saved, gain_vec):
    unit_rows, inv_scale, act_rows, upper_rows, swished, w_in_all, w_out_all = saved
    grad_branch = (0.5 * grad_resid).astype(jnp.bfloat16)
    grad_b_out = jnp.sum(grad_branch, axis=(0, 1), dtype=jnp.float32)
    grad_swished = jnp.einsum(
        "ild,cd->ilc", grad_branch, w_out_all, preferred_element_type=jnp.float32
    )
    grad_upper = (grad_swished * swish_slope(upper_rows)).astype(jnp.bfloat16)
    grad_act = jnp.einsum("ilc,dc->ild", grad_upper, w_in_all, preferred_element_type=jnp.float32)
    grad_w_in = jnp.einsum("ild,ilc->dc", act_rows, grad_upper, preferred_element_type=jnp.float32)
    grad_b_in = jnp.sum(grad_upper, axis=(0, 1), dtype=jnp.float32)
    grad_w_out = jnp.einsum("ilc,ild->cd", swished, grad_branch, preferred_element_type=jnp.float32)
    grad_w_in, grad_b_in, grad_w_out = (
        lax.psum_scatter(grad_w_in, "mp", scatter_dimension=1, tiled=True),
        lax.psum_scatter(grad_b_in, "mp", scatter_dimension=0, tiled=True),
        lax.psum_scatter(grad_w_out, "mp", scatter_dimension=0, tiled=True),
    )
    grad_in, grad_gain, grad_shift = norm_backward(grad_act, unit_rows, inv_scale, gain_vec)
    return (
        grad_resid + grad_in,
        (grad_w_in, grad_b_in, grad_w_out),
        (grad_gain, grad_shift, grad_b_out),
    )


def split_heads(rows_bf):
    frame_count = rows_bf.shape[0]
    return rows_bf.reshape(frame_count, rows_bf.shape[1] // HEAD, HEAD)


def item_scores(query_heads, key_heads, length):
    frame_count = query_heads.shape[0]
    scores = jnp.einsum(
        "qhe,khe->hqk", query_heads, key_heads, preferred_element_type=jnp.float32
    ) * (1.0 / math.sqrt(HEAD))
    visible = jnp.arange(frame_count) < length
    return jnp.where(visible[None, None, :], scores, -1e30)


def attend_forward(packed):
    query_rows, key_rows, value_rows, length = packed
    frame_count = query_rows.shape[0]
    scores = item_scores(split_heads(query_rows), split_heads(key_rows), length)
    row_max = jnp.max(scores, axis=-1, keepdims=True)
    shifted = jnp.exp(scores - row_max)
    row_total = jnp.sum(shifted, axis=-1, keepdims=True)
    attn_probs = (shifted / row_total).astype(jnp.bfloat16)
    mixed_rows = jnp.einsum(
        "hqk,khe->qhe", attn_probs, split_heads(value_rows), preferred_element_type=jnp.float32
    )
    return (
        mixed_rows.reshape(frame_count, -1).astype(jnp.bfloat16),
        (row_max + jnp.log(row_total))[..., 0],
    )


def attend_backward(packed):
    query_rows, key_rows, value_rows, grad_mixed, log_total, length = packed
    frame_count = query_rows.shape[0]
    query_heads = split_heads(query_rows)
    key_heads = split_heads(key_rows)
    value_heads = split_heads(value_rows)
    grad_heads = split_heads(grad_mixed)
    attn_probs = jnp.exp(item_scores(query_heads, key_heads, length) - log_total[..., None])
    grad_probs = jnp.einsum(
        "qhe,khe->hqk", grad_heads, value_heads, preferred_element_type=jnp.float32
    )
    grad_value = jnp.einsum(
        "hqk,qhe->khe",
        attn_probs.astype(jnp.bfloat16),
        grad_heads,
        preferred_element_type=jnp.float32,
    )
    row_dot = jnp.sum(attn_probs * grad_probs, axis=-1, keepdims=True)
    grad_scores = (attn_probs * (grad_probs - row_dot)).astype(jnp.bfloat16)
    scale_factor = 1.0 / math.sqrt(HEAD)
    grad_query = (
        jnp.einsum("hqk,khe->qhe", grad_scores, key_heads, preferred_element_type=jnp.float32)
        * scale_factor
    )
    grad_key = (
        jnp.einsum("hqk,qhe->khe", grad_scores, query_heads, preferred_element_type=jnp.float32)
        * scale_factor
    )
    return (
        grad_query.reshape(frame_count, -1).astype(jnp.bfloat16),
        grad_key.reshape(frame_count, -1).astype(jnp.bfloat16),
        grad_value.reshape(frame_count, -1).astype(jnp.bfloat16),
    )


def att_forward(resid, lengths, gain_vec, shift_vec, w_qkv, b_qv, w_out, b_out):
    normed, unit_rows, inv_scale = norm_forward(resid, gain_vec, shift_vec)
    act_rows = spread_rows(normed.astype(jnp.bfloat16))
    stacked = jnp.einsum("ild,kdc->kilc", act_rows, w_qkv, preferred_element_type=jnp.float32)
    query_rows = (stacked[0] + b_qv[0]).astype(jnp.bfloat16)
    key_rows = stacked[1].astype(jnp.bfloat16)
    value_rows = (stacked[2] + b_qv[1]).astype(jnp.bfloat16)
    mixed_rows, log_total = lax.map(attend_forward, (query_rows, key_rows, value_rows, lengths))
    branch = (
        collect_rows(
            jnp.einsum("ilc,cd->ild", mixed_rows, w_out, preferred_element_type=jnp.float32)
        )
        + b_out
    )
    return (
        branch,
        (unit_rows, inv_scale, act_rows, query_rows, key_rows, value_rows, mixed_rows, log_total),
    )


def att_backward(grad_resid, saved, lengths, gain_vec, w_qkv, w_out):
    unit_rows, inv_scale, act_rows, query_rows, key_rows, value_rows, mixed_rows, log_total = saved
    grad_branch = grad_resid.astype(jnp.bfloat16)
    grad_b_out = jnp.sum(grad_branch, axis=(0, 1), dtype=jnp.float32)
    grad_rows = spread_grads(grad_branch)
    grad_mixed = jnp.einsum(
        "ild,cd->ilc", grad_rows, w_out, preferred_element_type=jnp.float32
    ).astype(jnp.bfloat16)
    grad_w_out = jnp.einsum(
        "ilc,ild->cd", mixed_rows, grad_rows, preferred_element_type=jnp.float32
    )
    grad_query, grad_key, grad_value = lax.map(
        attend_backward, (query_rows, key_rows, value_rows, grad_mixed, log_total, lengths)
    )
    grad_stack = jnp.stack([grad_query, grad_key, grad_value])
    grad_act = collect_grads(
        jnp.einsum("kilc,kdc->ild", grad_stack, w_qkv, preferred_element_type=jnp.float32)
    )
    grad_w_qkv = jnp.einsum(
        "ild,kilc->kdc", act_rows, grad_stack, preferred_element_type=jnp.float32
    )
    grad_b_qv = jnp.stack(
        [
            jnp.sum(grad_query, axis=(0, 1), dtype=jnp.float32),
            jnp.sum(grad_value, axis=(0, 1), dtype=jnp.float32),
        ]
    )
    grad_in, grad_gain, grad_shift = norm_backward(grad_act, unit_rows, inv_scale, gain_vec)
    return (
        grad_resid + grad_in,
        (grad_w_qkv, grad_b_qv, grad_w_out),
        (grad_gain, grad_shift, grad_b_out),
    )


def pad_frames(signal, half_width):
    return jnp.pad(signal, ((0, 0), (half_width, half_width), (0, 0)))


def depthwise(signal, kernel):
    half_width = kernel.shape[0] // 2
    frame_count = signal.shape[1]
    padded = pad_frames(signal, half_width)
    summed = jnp.zeros_like(signal)
    for offset in range(kernel.shape[0]):
        summed = summed + padded[:, offset : offset + frame_count, :] * kernel[offset]
    return summed


def depthwise_back(grad_out, kernel):
    half_width = kernel.shape[0] // 2
    frame_count = grad_out.shape[1]
    padded = pad_frames(grad_out, half_width)
    summed = jnp.zeros_like(grad_out)
    for offset in range(kernel.shape[0]):
        start = 2 * half_width - offset
        summed = summed + padded[:, start : start + frame_count, :] * kernel[offset]
    return summed


def depthwise_weight(grad_out, signal, taps):
    half_width = taps // 2
    frame_count = signal.shape[1]
    padded = pad_frames(signal, half_width)
    return jnp.stack(
        [
            jnp.sum(grad_out * padded[:, offset : offset + frame_count, :], axis=(0, 1))
            for offset in range(taps)
        ]
    )


def conv_forward(
    resid, visible, gain_vec, shift_vec, w_in, b_in, w_depth, bn_scale, bn_shift, w_out, b_out
):
    normed, unit_rows, inv_scale = norm_forward(resid, gain_vec, shift_vec)
    act_rows = spread_rows(normed.astype(jnp.bfloat16))
    both_halves = (
        jnp.einsum("ild,kdc->kilc", act_rows, w_in, preferred_element_type=jnp.float32)
        + b_in[:, None, None, :]
    )
    logistic = jax.nn.sigmoid(both_halves[1])
    gated_rows = both_halves[0] * logistic * visible[..., None]
    depth_out = depthwise(gated_rows, w_depth)
    local_count = jnp.sum(visible)
    weighted = depth_out * visible[..., None]
    sum_vals, valid_count = lax.psum((jnp.sum(weighted, axis=(0, 1)), local_count), "dp")
    batch_mean = sum_vals / valid_count
    centred = depth_out - batch_mean
    batch_var = (
        lax.psum(jnp.sum(centred * centred * visible[..., None], axis=(0, 1)), "dp") / valid_count
    )
    inv_batch = lax.rsqrt(batch_var + EPS)
    normed_bn = centred * inv_batch * bn_scale + bn_shift
    swished = jax.nn.silu(normed_bn).astype(jnp.bfloat16)
    branch = (
        collect_rows(jnp.einsum("ilc,cd->ild", swished, w_out, preferred_element_type=jnp.float32))
        + b_out
    )
    saved = (
        unit_rows,
        inv_scale,
        act_rows,
        both_halves,
        logistic,
        gated_rows,
        centred,
        inv_batch,
        normed_bn,
        swished,
        valid_count,
    )
    return (branch, saved, batch_mean, batch_var, valid_count)


def conv_backward(grad_resid, saved, visible, gain_vec, w_in, w_depth, bn_scale, w_out):
    (
        unit_rows,
        inv_scale,
        act_rows,
        both_halves,
        logistic,
        gated_rows,
        centred,
        inv_batch,
        normed_bn,
        swished,
        valid_count,
    ) = saved
    grad_branch = grad_resid.astype(jnp.bfloat16)
    grad_b_out = jnp.sum(grad_branch, axis=(0, 1), dtype=jnp.float32)
    grad_rows = spread_grads(grad_branch)
    grad_swished = jnp.einsum("ild,cd->ilc", grad_rows, w_out, preferred_element_type=jnp.float32)
    grad_w_out = jnp.einsum("ilc,ild->cd", swished, grad_rows, preferred_element_type=jnp.float32)
    grad_normed = grad_swished * swish_slope(normed_bn)
    unit_bn = centred * inv_batch
    grad_scale = jnp.sum(grad_normed * unit_bn, axis=(0, 1))
    grad_shift_bn = jnp.sum(grad_normed, axis=(0, 1))
    grad_unit = grad_normed * bn_scale
    sum_unit, sum_cross = lax.psum(
        (jnp.sum(grad_unit, axis=(0, 1)), jnp.sum(grad_unit * centred, axis=(0, 1))), "dp"
    )
    inv_cube = inv_batch * inv_batch * inv_batch
    grad_depth_out = (
        grad_unit * inv_batch
        - visible[..., None] * (inv_batch * sum_unit + inv_cube * sum_cross * centred) / valid_count
    )
    grad_gated = depthwise_back(grad_depth_out, w_depth) * visible[..., None]
    grad_w_depth = depthwise_weight(grad_depth_out, gated_rows, w_depth.shape[0])
    grad_both = jnp.stack(
        [grad_gated * logistic, grad_gated * both_halves[0] * logistic * (1.0 - logistic)]
    ).astype(jnp.bfloat16)
    grad_act = collect_grads(
        jnp.einsum("kilc,kdc->ild", grad_both, w_in, preferred_element_type=jnp.float32)
    )
    grad_w_in = jnp.einsum("ild,kilc->kdc", act_rows, grad_both, preferred_element_type=jnp.float32)
    grad_b_in = jnp.sum(grad_both, axis=(1, 2), dtype=jnp.float32)
    grad_in, grad_gain, grad_shift = norm_backward(grad_act, unit_rows, inv_scale, gain_vec)
    return (
        grad_resid + grad_in,
        (grad_w_in, grad_b_in, grad_w_depth, grad_scale, grad_shift_bn, grad_w_out),
        (grad_gain, grad_shift, grad_b_out),
    )


def shards(
    frames,
    lengths,
    mask_flags,
    mask_embed,
    ffa_gain,
    ffa_shift,
    ffa_w_in,
    ffa_b_in,
    ffa_w_out,
    ffa_b_out,
    att_gain,
    att_shift,
    att_w_qkv,
    att_b_qv,
    att_w_out,
    att_b_out,
    conv_gain,
    conv_shift,
    conv_w_in,
    conv_b_in,
    conv_w_depth,
    batch_scale,
    batch_shift,
    running_mean,
    running_var,
    conv_w_out,
    conv_b_out,
    ffb_gain,
    ffb_shift,
    ffb_w_in,
    ffb_b_in,
    ffb_w_out,
    ffb_b_out,
    final_gain,
    final_shift,
    cotangent,
):
    frame_total = frames.shape[1] * lax.axis_size("mp")
    visible = (jnp.arange(frame_total)[None, :] < lengths[:, None]).astype(jnp.float32)
    flag_rows = mask_flags.astype(jnp.float32)
    resid_a = frames.astype(jnp.float32) + flag_rows[..., None] * mask_embed
    branch, saved_ffa = ffn_forward(
        resid_a, ffa_gain, ffa_shift, ffa_w_in, ffa_b_in, ffa_w_out, ffa_b_out
    )
    resid_b = resid_a + 0.5 * branch
    branch, saved_att = att_forward(
        resid_b, lengths, att_gain, att_shift, att_w_qkv, att_b_qv, att_w_out, att_b_out
    )
    resid_c = resid_b + branch
    branch, saved_conv, batch_mean, batch_var, valid_count = conv_forward(
        resid_c,
        visible,
        conv_gain,
        conv_shift,
        conv_w_in,
        conv_b_in,
        conv_w_depth,
        batch_scale,
        batch_shift,
        conv_w_out,
        conv_b_out,
    )
    resid_d = resid_c + branch
    branch, saved_ffb = ffn_forward(
        resid_d, ffb_gain, ffb_shift, ffb_w_in, ffb_b_in, ffb_w_out, ffb_b_out
    )
    resid_e = resid_d + 0.5 * branch
    layer_out, unit_out, inv_out = norm_forward(resid_e, final_gain, final_shift)
    grad_resid, grad_final_gain, grad_final_shift = norm_backward(
        cotangent.astype(jnp.float32), unit_out, inv_out, final_gain
    )
    grad_resid, ffb_mats, ffb_vecs = ffn_backward(grad_resid, saved_ffb, ffb_gain)
    grad_resid, conv_mats, conv_vecs = conv_backward(
        grad_resid, saved_conv, visible, conv_gain, conv_w_in, conv_w_depth, batch_scale, conv_w_out
    )
    grad_resid, att_mats, att_vecs = att_backward(
        grad_resid, saved_att, lengths, att_gain, att_w_qkv, att_w_out
    )
    grad_resid, ffa_mats, ffa_vecs = ffn_backward(grad_resid, saved_ffa, ffa_gain)
    grad_embed = jnp.sum(grad_resid * flag_rows[..., None], axis=(0, 1))
    summed_mats = lax.psum(
        (
            ffa_mats[0],
            ffa_mats[1],
            ffa_mats[2],
            att_mats[0],
            att_mats[1],
            att_mats[2],
            conv_mats[0],
            conv_mats[1],
            conv_mats[2],
            conv_mats[3],
            conv_mats[4],
            conv_mats[5],
            ffb_mats[0],
            ffb_mats[1],
            ffb_mats[2],
        ),
        "dp",
    )
    summed_vecs = lax.psum(
        (
            grad_embed,
            ffa_vecs[0],
            ffa_vecs[1],
            ffa_vecs[2],
            att_vecs[0],
            att_vecs[1],
            att_vecs[2],
            conv_vecs[0],
            conv_vecs[1],
            conv_vecs[2],
            ffb_vecs[0],
            ffb_vecs[1],
            ffb_vecs[2],
            grad_final_gain,
            grad_final_shift,
        ),
        ("dp", "mp"),
    )
    new_mean = 0.9 * running_mean + 0.1 * batch_mean
    new_var = 0.9 * running_var + 0.1 * batch_var * valid_count / (valid_count - 1.0)
    return (
        layer_out,
        grad_resid,
        summed_vecs[0],
        summed_vecs[1],
        summed_vecs[2],
        summed_mats[0],
        summed_mats[1],
        summed_mats[2],
        summed_vecs[3],
        summed_vecs[4],
        summed_vecs[5],
        summed_mats[3],
        summed_mats[4],
        summed_mats[5],
        summed_vecs[6],
        summed_vecs[7],
        summed_vecs[8],
        summed_mats[6],
        summed_mats[7],
        summed_mats[8],
        summed_mats[9],
        summed_mats[10],
        summed_mats[11],
        summed_vecs[9],
        summed_vecs[10],
        summed_vecs[11],
        summed_mats[12],
        summed_mats[13],
        summed_mats[14],
        summed_vecs[12],
        summed_vecs[13],
        summed_vecs[14],
        new_mean,
        new_var,
    )


def solution(mesh):
    return jax.shard_map(
        shards,
        mesh=mesh,
        in_specs=(
            P("dp", "mp", None),
            P("dp"),
            P("dp", "mp"),
            P(),
            P(),
            P(),
            P(None, "mp"),
            P("mp"),
            P("mp", None),
            P(),
            P(),
            P(),
            P(None, None, "mp"),
            P(None, "mp"),
            P("mp", None),
            P(),
            P(),
            P(),
            P(None, None, "mp"),
            P(None, "mp"),
            P(None, "mp"),
            P("mp"),
            P("mp"),
            P("mp"),
            P("mp"),
            P("mp", None),
            P(),
            P(),
            P(),
            P(None, "mp"),
            P("mp"),
            P("mp", None),
            P(),
            P(),
            P(),
            P("dp", "mp", None),
        ),
        out_specs=(
            P("dp", "mp", None),
            P("dp", "mp", None),
            P(),
            P(),
            P(),
            P(None, "mp"),
            P("mp"),
            P("mp", None),
            P(),
            P(),
            P(),
            P(None, None, "mp"),
            P(None, "mp"),
            P("mp", None),
            P(),
            P(),
            P(),
            P(None, None, "mp"),
            P(None, "mp"),
            P(None, "mp"),
            P("mp"),
            P("mp"),
            P("mp", None),
            P(),
            P(),
            P(),
            P(None, "mp"),
            P("mp"),
            P("mp", None),
            P(),
            P(),
            P(),
            P("mp"),
            P("mp"),
        ),
        check_vma=False,
    )
```

profile of v0, /device:TPU:0, one launch (start us, length us, event | category | flops | bytes accessed | tf_op | source)
XLA Modules:
  0.0 2481.7 jit_solution(6725460691523690842)
XLA Ops:
  24.2 70.3 %all-gather.11.cloned.1.call-done = bf16[1024,4096]{1,0:T(8,128)(2,1)} async-done(((bf16[1024,512]{1,0:T(8,128)(2,1)}), bf16[1024,4096]{1,0:T(8,128)(2,1)}) %all-gather.11.cloned.1.call-update) | async-done | bytes 8388624 | tf_op jit(solution)/shard_map/all_gather | solution.py:57
  103.9 72.9 %all-gather.13.cloned.1.call-done = bf16[4096,1024]{1,0:T(8,128)(2,1)} async-done(((bf16[512,1024]{1,0:T(8,128)(2,1)}), bf16[4096,1024]{1,0:T(8,128)(2,1)}) %all-gather.13.cloned.1.call-update) | async-done | bytes 8388624 | tf_op jit(solution)/shard_map/all_gather | solution.py:59
  188.6 67.7 %all-gather.15.cloned.1.call-done = bf16[2,1664,1024]{2,1,0:T(8,128)(2,1)} async-done(((bf16[2,208,1024]{2,1,0:T(8,128)(2,1)}), bf16[2,1664,1024]{2,1,0:T(8,128)(2,1)}) %all-gather.15.cloned.1.call-update) | async-done | bytes 6815760 | tf_op jit(solution)/shard_map/all_gather | solution.py:38
  272.8 46.3 %while.26 = (s32[]{:T(128)}, bf16[2,1664,128]{1,2,0:T(8,128)(2,1)}, f32[2,2,1664]{2,1,0:T(2,128)S(1)}, bf16[2,1664,128]{1,2,0:T(8,128)(2,1)}, s32[2]{0:T(128)S(1...) while((s32[]{:T(128)}, bf16[2,1664,128]{1,2,0:T(8,128)(2,1)}, ...), condition=%wide.region_7.8_spmd, body=%wide.region_4.7_spmd.sunk | while | flops 1484339584 | bytes 71678584 | solution.py:168
  327.5 137.9 %reduce-scatter.9.cloned.1.call-done = f32[2,208,1024]{2,1,0:T(8,128)} async-done(((f32[2,1664,1024]{2,1,0:T(8,128)}), f32[2,208,1024]{2,1,0:T(8,128)}) %reduce-scatter.9.cloned.1.call-update) | async-done | bytes 1703952 | tf_op jit(solution)/shard_map/reduce_scatter | solution.py:42
  470.8 66.4 %all-gather.17.cloned.1.call-done = bf16[2,1664,1024]{2,1,0:T(8,128)(2,1)} async-done(((bf16[2,208,1024]{2,1,0:T(8,128)(2,1)}), bf16[2,1664,1024]{2,1,0:T(8,128)(2,1)}) %all-gather.17.cloned.1.call-update) | async-done | bytes 6815760 | tf_op jit(solution)/shard_map/all_gather | solution.py:38
  605.6 121.4 %reduce-scatter.11.cloned.1.call-done = f32[2,208,1024]{2,1,0:T(8,128)} async-done(((f32[2,1664,1024]{2,1,0:T(8,128)}), f32[2,208,1024]{2,1,0:T(8,128)}) %reduce-scatter.11.cloned.1.call-update) | async-done | bytes 1703952 | tf_op jit(solution)/shard_map/reduce_scatter | solution.py:42
  731.3 77.5 %all-gather.19.cloned.1.call-done = bf16[1024,4096]{1,0:T(8,128)(2,1)} async-done(((bf16[1024,512]{1,0:T(8,128)(2,1)}), bf16[1024,4096]{1,0:T(8,128)(2,1)}) %all-gather.19.cloned.1.call-update) | async-done | bytes 8388624 | tf_op jit(solution)/shard_map/all_gather | solution.py:57
  819.7 71.4 %all-gather.21.cloned.1.call-done = bf16[4096,1024]{1,0:T(8,128)(2,1)} async-done(((bf16[512,1024]{1,0:T(8,128)(2,1)}), bf16[4096,1024]{1,0:T(8,128)(2,1)}) %all-gather.21.cloned.1.call-update) | async-done | bytes 8388624 | tf_op jit(solution)/shard_map/all_gather | solution.py:59
  925.2 67.7 %all-gather.23.cloned.1.call-done = bf16[2,1664,1024]{2,1,0:T(8,128)(2,1)} async-done(((bf16[2,208,1024]{2,1,0:T(8,128)(2,1)}), bf16[2,1664,1024]{2,1,0:T(8,128)(2,1)}) %all-gather.23.cloned.1.call-update) | async-done | bytes 6815760 | tf_op jit(solution)/shard_map/all_gather | solution.py:46
  1034.9 136.1 %reduce-scatter.13.cloned.1.call-done = f32[2,208,1024]{2,1,0:T(8,128)} async-done(((f32[2,1664,1024]{2,1,0:T(8,128)}), f32[2,208,1024]{2,1,0:T(8,128)}) %reduce-scatter.13.cloned.1.call-update) | async-done | bytes 1703952 | tf_op jit(solution)/shard_map/reduce_scatter | solution.py:50
  1176.8 67.5 %all-gather.25.cloned.1.call-done = bf16[2,1664,1024]{2,1,0:T(8,128)(2,1)} async-done(((bf16[2,208,1024]{2,1,0:T(8,128)(2,1)}), bf16[2,1664,1024]{2,1,0:T(8,128)(2,1)}) %all-gather.25.cloned.1.call-update) | async-done | bytes 6815760 | tf_op jit(solution)/shard_map/all_gather | solution.py:46
  1252.0 141.7 %while.27 = (s32[]{:T(128)}, bf16[2,1664,128]{1,2,0:T(8,128)(2,1)}, bf16[2,1664,128]{2,1,0:T(8,128)(2,1)}, bf16[2,1664,128]{1,2,0:T(8,128)(2,1)}, bf16[2,1664,12...) while((s32[]{:T(128)}, bf16[2,1664,128]{1,2,0:T(8,128)(2,1)}, ...), condition=%wide.region_35.36_spmd, body=%wide.region_33.35_spmd.sunk | while | flops 3595090432 | bytes 211358224 | solution.py:192
  1281.6 18.8 multiply_convert_fusion.20
  1352.3 18.8 multiply_convert_fusion.20
  1428.9 113.5 %reduce-scatter.15.cloned.1.call-done = f32[2,208,1024]{2,1,0:T(8,128)} async-done(((f32[2,1664,1024]{2,1,0:T(8,128)}), f32[2,208,1024]{2,1,0:T(8,128)}) %reduce-scatter.15.cloned.1.call-update) | async-done | bytes 1703952 | tf_op jit(solution)/shard_map/reduce_scatter | solution.py:50
  1603.3 108.1 %reduce-scatter.23.cloned.1.call-done = f32[512,1024]{1,0:T(8,128)} async-done(((f32[4096,1024]{1,0:T(8,128)}), f32[512,1024]{1,0:T(8,128)}) %reduce-scatter.23.cloned.1.call-update) | async-done | bytes 2097168 | tf_op jit(solution)/shard_map/reduce_scatter | solution.py:85
  1711.4 168.8 %reduce-scatter.21.cloned.1.call-done = f32[1024,512]{1,0:T(8,128)} async-done(((f32[1024,4096]{1,0:T(8,128)}), f32[1024,512]{1,0:T(8,128)}) %reduce-scatter.21.cloned.1.call-update) | async-done | bytes 2097168 | tf_op jit(solution)/shard_map/reduce_scatter | solution.py:83
  1880.2 168.8 %reduce-scatter.19.cloned.1.call-done = f32[512,1024]{1,0:T(8,128)} async-done(((f32[4096,1024]{1,0:T(8,128)}), f32[512,1024]{1,0:T(8,128)}) %reduce-scatter.19.cloned.1.call-update) | async-done | bytes 2097168 | tf_op jit(solution)/shard_map/reduce_scatter | solution.py:85
  2049.0 168.8 %reduce-scatter.17.cloned.1.call-done = f32[1024,512]{1,0:T(8,128)} async-done(((f32[1024,4096]{1,0:T(8,128)}), f32[1024,512]{1,0:T(8,128)}) %reduce-scatter.17.cloned.1.call-update) | async-done | bytes 2097168 | tf_op jit(solution)/shard_map/reduce_scatter | solution.py:83
  2229.5 26.0 %all-reduce.5 = (f32[4096]{0:T(1024)S(1)}, f32[4096]{0:T(1024)S(1)}) all-reduce(f32[4096]{0:T(1024)S(1)} %get-tuple-element.436, f32[4096]{0:T(1024)S(1)} %copy-done.83), channel_id=7, replica_groups=mesh['dp'=4,'mp'=8] {'mp'}, use_global_device_ids=true, to_apply=%region_50.51.clone | all-reduce | flops 8192 | bytes 65536
  2255.6 17.6 all-reduce.6
  2283.6 39.4 %all-reduce.4 = (f32[1024]{0:T(1024)}, f32[1024]{0:T(1024)}, f32[1024]{0:T(1024)}, f32[1024]{0:T(1024)}, f32[1024]{0:T(1024)}, /*index=5*/f32[1024]{0:T(1024)}, ...) all-reduce(f32[1024]{0:T(1024)S(1)} %get-tuple-element.373, ...), channel_id=1, replica_groups=mesh['dp'=4,'mp'=8] {'dp','mp'}, use_global_device_ids=true, to_apply=%region_42.43 | all-reduce | flops 15360 | bytes 122880 | tf_op jit(solution)/shard_map/psum | solution.py:447
  2323.0 137.2 %all-reduce.12.cloned.1.call-done = (f32[1024,512]{1,0:T(8,128)}, f32[512,1024]{1,0:T(8,128)}, f32[3,1024,128]{1,2,0:T(8,128)}, f32[128,1024]{1,0:T(8,128)}, f32...) async-done(((f32[1024,512]{1,0:T(8,128)}, f32[512,1024]{1,0:T(8,128)}, f32[3,1024,128]{1,2,0:T(8,128)}, ...) | async-done | bytes 12058640 | tf_op jit(solution)/shard_map/psum | solution.py:427
  (613 shorter events, 519.7 us)
Async XLA Ops:
  7.2 249.1 %copy-start = (bf16[3,1024,128]{2,1,0:T(8,128)(2,1)S(1)}, bf16[3,1024,128]{2,1,0:T(8,128)(2,1)}, u32[]{:S(2)}) copy-start(bf16[3,1024,128]{2,1,0:T(8,128)(2,1)} %param.52) | copy-start | bytes 2359300
  7.3 87.2 %all-gather.11.cloned.1.call-start = ((), (), s32[]{:S(2)}) async-start(), calls=%async_computation.8 | async-start | bytes 9437184 | tf_op jit(solution)/shard_map/all_gather | solution.py:57
  8.0 168.7 %all-gather.13.cloned.1.call-start = ((), (), s32[]{:S(2)}) async-start(), calls=%async_computation.9 | async-start | bytes 9437184 | tf_op jit(solution)/shard_map/all_gather | solution.py:59
  8.8 247.5 %all-gather.15.cloned.1.call-start = ((), (), s32[]{:S(2)}) async-start(), calls=%async_computation.10 | async-start | bytes 7667712 | tf_op jit(solution)/shard_map/all_gather | solution.py:38
  8.9 167.9 %copy-start.63 = (f32[2,208]{1,0:T(2,128)}, f32[2,208]{1,0:T(2,128)S(1)}, u32[]{:S(2)}) copy-start(f32[2,208]{1,0:T(2,128)S(1)} %convert_element_type.180) | copy-start | bytes 4996
  23.3 153.4 %copy-start.81 = (f32[8,1,512]{2,1,0:T(1,128)}, f32[8,1,512]{2,1,0:T(1,128)S(1)}, u32[]{:S(2)}) copy-start(f32[8,1,512]{2,1,0:T(1,128)S(1)} %convert_element_type.211) | copy-start | bytes 49156
  24.2 152.5 %copy-start.186 = (f32[1024]{0:T(1024)S(1)}, f32[1024]{0:T(1024)}, u32[]{:S(2)}) copy-start(f32[1024]{0:T(1024)} %param.49) | copy-start | bytes 12292
  188.6 276.9 %reduce-scatter.9.cloned.1.call-start = ((), (), s32[]{:S(2)}) async-start(), calls=%async_computation.11 | async-start | bytes 15335424 | tf_op jit(solution)/shard_map/reduce_scatter | solution.py:42
  327.5 138.0 %copy-start.6 = (f32[2,208,1024]{2,1,0:T(8,128)S(1)}, f32[2,208,1024]{2,1,0:T(8,128)}, u32[]{:S(2)}) copy-start(f32[2,208,1024]{2,1,0:T(8,128)} %copy-done.5) | copy-start | bytes 5111812
  327.5 138.0 %copy-start.167 = (f32[1024]{0:T(1024)S(1)}, f32[1024]{0:T(1024)}, u32[]{:S(2)}) copy-start(f32[1024]{0:T(1024)} %param.55) | copy-start | bytes 12292
  327.5 209.7 %all-gather.17.cloned.1.call-start = ((), (), s32[]{:S(2)}) async-start(), calls=%async_computation.12 | async-start | bytes 7667712 | tf_op jit(solution)/shard_map/all_gather | solution.py:38
  469.7 257.3 %reduce-scatter.11.cloned.1.call-start = ((), (), s32[]{:S(2)}) async-start(), calls=%async_computation.13 | async-start | bytes 15335424 | tf_op jit(solution)/shard_map/reduce_scatter | solution.py:42
  543.8 467.7 %copy-start.1 = (f32[2,1664,128]{2,1,0:T(8,128)}, f32[2,1664,128]{2,1,0:T(8,128)S(1)}, u32[]{:S(2)}) copy-start(f32[2,1664,128]{2,1,0:T(8,128)S(1)} %multiply_multiply_fusion) | copy-start | bytes 5111812
  589.8 219.0 %all-gather.19.cloned.1.call-start = ((), (), s32[]{:S(2)}) async-start(), calls=%async_computation.14 | async-start | bytes 9437184 | tf_op jit(solution)/shard_map/all_gather | solution.py:57
  590.6 300.5 %all-gather.21.cloned.1.call-start = ((), (), s32[]{:S(2)}) async-start(), calls=%async_computation.15 | async-start | bytes 9437184 | tf_op jit(solution)/shard_map/all_gather | solution.py:59
  591.3 401.6 %all-gather.23.cloned.1.call-start = ((), (), s32[]{:S(2)}) async-start(), calls=%async_computation.16 | async-start | bytes 7667712 | tf_op jit(solution)/shard_map/all_gather | solution.py:46
  925.2 245.8 %reduce-scatter.13.cloned.1.call-start = ((), (), s32[]{:S(2)}) async-start(), calls=%async_computation.17 | async-start | bytes 15335424 | tf_op jit(solution)/shard_map/reduce_scatter | solution.py:50
  1034.9 209.4 %all-gather.25.cloned.1.call-start = ((), (), s32[]{:S(2)}) async-start(), calls=%async_computation.18 | async-start | bytes 7667712 | tf_op jit(solution)/shard_map/all_gather | solution.py:46
  1176.7 365.7 %reduce-scatter.15.cloned.1.call-start = ((), (), s32[]{:S(2)}) async-start(), calls=%async_computation.19 | async-start | bytes 15335424 | tf_op jit(solution)/shard_map/reduce_scatter | solution.py:50
  1404.5 306.9 %reduce-scatter.23.cloned.1.call-start = ((), (), s32[]{:S(2)}) async-start(), calls=%async_computation.23 | async-start | bytes 18874368 | tf_op jit(solution)/shard_map/reduce_scatter | solution.py:85
  1416.9 463.3 %reduce-scatter.21.cloned.1.call-start = ((), (), s32[]{:S(2)}) async-start(), calls=%async_computation.22 | async-start | bytes 18874368 | tf_op jit(solution)/shard_map/reduce_scatter | solution.py:83
  1428.9 620.2 %reduce-scatter.19.cloned.1.call-start = ((), (), s32[]{:S(2)}) async-start(), calls=%async_computation.21 | async-start | bytes 18874368 | tf_op jit(solution)/shard_map/reduce_scatter | solution.py:85
  1558.9 658.9 %reduce-scatter.17.cloned.1.call-start = ((), (), s32[]{:S(2)}) async-start(), calls=%async_computation.20 | async-start | bytes 18874368 | tf_op jit(solution)/shard_map/reduce_scatter | solution.py:83
  1582.2 878.0 %all-reduce.12.cloned.1.call-start = ((), (), s32[]{:S(2)}) async-start(), calls=%async_computation.24 | async-start | bytes 24117248 | tf_op jit(solution)/shard_map/psum | solution.py:427
  (197 other events, 4649.1 us)
Sparse Core Ops, SparseCore 0:
  9.7 84.7 all-gather.10
  96.1 80.5 all-gather.12
  188.7 67.5 all-gather.14
  327.6 137.7 reduce-scatter.8
  469.8 67.3 all-gather.16
  590.0 137.0 reduce-scatter.10
  728.6 80.1 all-gather.18
  810.4 80.5 all-gather.20
  925.3 67.5 all-gather.22
  1035.0 135.9 reduce-scatter.12
  1176.8 67.3 all-gather.24
  1404.6 137.7 reduce-scatter.14
  1544.8 166.5 reduce-scatter.22
  1713.6 166.5 reduce-scatter.20
  1882.4 166.5 reduce-scatter.18
  2051.3 166.5 reduce-scatter.16
  2223.6 236.6 all-reduce.11
where the time goes:
time: 2490 us; the launch traced here: 2480 us
  waiting for transfers between devices  1820 us (73%)
  matrix products  306 us (12%)
  blocking collectives  140 us (6%)
  other arithmetic  123 us (5%)
  local copies, waits for them, and re-layouts  68.2 us (3%)
    reduce_scatter x2, waiting for transfers between devices, ffn_backward(): lax.psum_scatter(grad_w_in, 'mp', scatter_dimension=1, tiled=True)  338 us
    reduce_scatter x2, waiting for transfers between devices, ffn_backward(): lax.psum_scatter(grad_w_out, 'mp', scatter_dimension=0, tiled=True)  277 us
    reduce_scatter x2, waiting for transfers between devices, collect_rows(): return lax.psum_scatter(partial_rows, 'mp', scatter_dimension=1, tiled=True)  259 us
    reduce_scatter x2, waiting for transfers between devices, collect_grads(): return lax.psum_scatter(partial_rows, 'mp', scatter_dimension=1, tiled=True)  250 us
    all_gather x2, waiting for transfers between devices, ffn_forward(): lax.all_gather(w_in, 'mp', axis=1, tiled=True)  148 us
    all_gather x2, waiting for transfers between devices, ffn_forward(): lax.all_gather(w_out, 'mp', axis=0, tiled=True)  144 us
    psum x1, waiting for transfers between devices, shards(): lax.psum((ffa_mats[0], ffa_mats[1], ffa_mats[2], att_mats[0], att_mats[1]...  137 us
    all_gather x2, waiting for transfers between devices, spread_grads(): return lax.all_gather(local_rows, 'mp', axis=1, tiled=True)  135 us
  transfers between devices with their start and end apart: 17, of which 17 were waited for; matrix products, arithmetic and copies ran while one was open for 5% of the time, Pallas kernels for 0%

commit v1 on v0

v1 whole, which is shorter than its diff:
```python
import functools
import math

import jax
import jax.numpy as jnp
from jax import lax
from jax.experimental import pallas as pl
from jax.experimental.pallas import tpu as pltpu
from jax.sharding import PartitionSpec as P

HEAD = 64
EPS = 1e-05
BF = jnp.bfloat16
F32 = jnp.float32
LOG2E = math.log2(math.e)


def dot_nn(left, right):
    return lax.dot_general(left, right, (((1,), (0,)), ((), ())), preferred_element_type=F32)


def dot_nt(left, right):
    return lax.dot_general(left, right, (((1,), (1,)), ((), ())), preferred_element_type=F32)


def dot_tn(left, right):
    return lax.dot_general(left, right, (((0,), (0,)), ((), ())), preferred_element_type=F32)


def swap(values, axis, bit):
    count = lax.axis_size(axis)
    return lax.ppermute(values, axis, [(i, i ^ bit) for i in range(count)])


def bits_of(count):
    return [1 << k for k in range(count.bit_length() - 1)]


def norm_forward(values, gain_vec, shift_vec):
    row_mean = jnp.mean(values, axis=-1, keepdims=True)
    centred = values - row_mean
    inv_scale = lax.rsqrt(jnp.mean(centred * centred, axis=-1, keepdims=True) + EPS)
    unit_rows = centred * inv_scale
    return (unit_rows * gain_vec + shift_vec, unit_rows, inv_scale)


def norm_backward(grad_out, unit_rows, inv_scale, gain_vec):
    scaled = grad_out * gain_vec
    grad_in = inv_scale * (
        scaled
        - jnp.mean(scaled, axis=-1, keepdims=True)
        - unit_rows * jnp.mean(scaled * unit_rows, axis=-1, keepdims=True)
    )
    return (
        grad_in,
        jnp.sum(grad_out * unit_rows, axis=0, keepdims=True),
        jnp.sum(grad_out, axis=0, keepdims=True),
    )


def swish_slope(values):
    logistic = jax.nn.sigmoid(values)
    return logistic * (1.0 + values * (1.0 - logistic))


def split_halves(local):
    odd = lax.axis_index("mp") % 2
    first = lax.dynamic_index_in_dim(local, odd, 0, keepdims=False)
    second = lax.dynamic_index_in_dim(local, 1 - odd, 0, keepdims=False)
    return first, second


def send_halves(first, second):
    count = lax.axis_size("mp")
    group = count // 2
    straight = [(i, i // 2 + (group if i % 2 else 0)) for i in range(count)]
    crossed = [(i, i // 2 + (0 if i % 2 else group)) for i in range(count)]
    return lax.ppermute(first, "mp", straight), lax.ppermute(second, "mp", crossed)


def join_halves(got_a, got_b):
    low_half = lax.axis_index("mp") < lax.axis_size("mp") // 2
    lower = jnp.where(low_half, got_a, got_b)
    upper = jnp.where(low_half, got_b, got_a)
    return jnp.concatenate([lower, upper], axis=0)


def send_back(rows):
    count = lax.axis_size("mp")
    group = count // 2
    half = lax.axis_index("mp") // group
    frames = rows.shape[0] // 2
    lower, upper = rows[:frames], rows[frames:]
    straight = [(i // 2 + (group if i % 2 else 0), i) for i in range(count)]
    crossed = [(i // 2 + (0 if i % 2 else group), i) for i in range(count)]
    return (
        lax.ppermute(jnp.where(half == 0, lower, upper), "mp", straight),
        lax.ppermute(jnp.where(half == 0, upper, lower), "mp", crossed),
    )


def join_back(got_a, got_b):
    even = lax.axis_index("mp") % 2 == 0
    return jnp.stack([jnp.where(even, got_a, got_b), jnp.where(even, got_b, got_a)]).astype(F32)


hold = lax.optimization_barrier


def rounds_fit():
    return lax.axis_size("dp") == 4 and lax.axis_size("mp") == 8


def add_rounded(one, two):
    return (one.astype(F32) + two.astype(F32)).astype(BF)


def reordered(parts, index):
    count = parts.shape[0]
    return jnp.concatenate(
        [lax.dynamic_slice_in_dim(parts, k ^ index, 1, axis=0) for k in range(count)], axis=0
    )


def joined_z(parts):
    stacked = jnp.stack([parts[r] for r in sorted(parts)])
    ordered = jnp.moveaxis(reordered(stacked, lax.axis_index("mp") // 2), 0, 1)
    return ordered.reshape(-1, *ordered.shape[2:])


def spread_z(piece):
    parts = {0: piece}
    for bit in reversed(bits_of(lax.axis_size("mp"))[1:]):
        for index in list(parts):
            parts[index | bit] = swap(parts[index], "mp", bit)
    return parts


def spread_dp(pair):
    count = lax.axis_size("dp")
    if count != 4:
        for bit in bits_of(count):
            pair = jnp.concatenate([pair, swap(pair, "dp", bit)], axis=1)
        return pair
    by_x, by_y = hold((swap(pair, "dp", 1), swap(pair, "dp", 2)))
    both = jnp.stack([swap(by_y[0], "dp", 1), swap(by_x[1], "dp", 2)])
    return jnp.concatenate([pair, by_x, by_y, both], axis=1)


def spread_small(small):
    for bit in bits_of(lax.axis_size("mp")):
        small = jnp.concatenate([small, swap(small, "mp", bit)], axis=0)
    return small


def spread_rounds(piece, middle, late, halves, far_weight, extras):
    far_bit = lax.axis_size("mp") // 2
    if not rounds_fit():
        parts = spread_z(piece)
        near, far = (
            spread_dp(
                jnp.concatenate([parts[r] for r in sorted(parts) if (r & far_bit) == want], axis=1)
            )
            for want in (0, far_bit)
        )
        blocks = (near, swap(near, "mp", 1), far, swap(far, "mp", 1))
        return (
            blocks,
            joined_z(spread_z(middle)),
            joined_z(spread_z(late)),
            send_halves(*halves),
            swap(far_weight, "mp", far_bit),
            (spread_small(extras[0]), *extras[1:]),
        )
    small, rest = extras[0], list(extras[1:])
    near, far, middle, got, *rest = hold(
        (
            swap(piece, "mp", 2),
            swap(piece, "mp", 4),
            middle,
            swap(small, "mp", 1),
            *rest,
        )
    )
    small = jnp.concatenate([small, got], axis=0)
    part_a = jnp.concatenate([piece, near], axis=1)
    a_x, a_y, far_near, mid_near, mid_far, late, far_weight, got = hold(
        (
            swap(part_a, "dp", 1),
            swap(part_a, "dp", 2),
            swap(far, "mp", 2),
            swap(middle, "mp", 2),
            swap(middle, "mp", 4),
            late,
            far_weight,
            swap(small, "mp", 2),
        )
    )
    small = jnp.concatenate([small, got], axis=0)
    part_b = jnp.concatenate([far, far_near], axis=1)
    b_x, b_y, a_0, a_1, mid_both, late_near, late, far_weight, got, *halves = hold(
        (
            swap(part_b, "dp", 1),
            swap(part_b, "dp", 2),
            swap(a_y[0], "dp", 1),
            swap(a_x[1], "dp", 2),
            swap(mid_far, "mp", 2),
            swap(late, "mp", 2),
            late,
            swap(far_weight, "mp", 4),
            swap(small, "mp", 4),
            *halves,
        )
    )
    small = jnp.concatenate([small, got], axis=0)
    all_a = jnp.concatenate([part_a, a_x, a_y, jnp.stack([a_0, a_1])], axis=1)
    b_0, b_1, other_a, late, *halves = hold(
        (
            swap(b_y[0], "dp", 1),
            swap(b_x[1], "dp", 2),
            swap(all_a, "mp", 1),
            late,
            *send_halves(*halves),
        )
    )
    all_b = jnp.concatenate([part_b, b_x, b_y, jnp.stack([b_0, b_1])], axis=1)
    return (
        (all_a, other_a, all_b, swap(all_b, "mp", 1)),
        joined_z({0: middle, 2: mid_near, 4: mid_far, 6: mid_both}),
        (late, late_near),
        halves,
        far_weight,
        (small, *rest),
    )


def z_groups():
    count = lax.axis_size("mp")
    return [list(range(core, count, 2)) for core in range(2)]


def collect_z_relative(parts):
    live = {2 * k: parts[k] for k in range(parts.shape[0])}
    for bit in bits_of(lax.axis_size("mp"))[1:]:
        for index in [r for r in live if r & bit]:
            live[index ^ bit] = add_rounded(live[index ^ bit], swap(live.pop(index), "mp", bit))
    return live[0]


def halve_z(parts, bit):
    return add_rounded(parts[0::2], swap(parts[1::2], "mp", bit))


def collect_dp(pair):
    for bit in reversed(bits_of(lax.axis_size("dp"))):
        rows = pair.shape[1] // 2
        pair = add_rounded(pair[:, :rows], swap(pair[:, rows:], "dp", bit))
    return pair


def corners(parts):
    half = parts[3].shape[0] // 2
    return swap(parts[3][:half], "dp", 1), swap(parts[3][half:], "dp", 2)


def sides(parts, to_x, to_y):
    half = parts[0].shape[0] // 2
    via_x = jnp.concatenate([parts[1][:half], add_rounded(parts[1][half:], to_y)], axis=0)
    via_y = jnp.concatenate([add_rounded(parts[2][:half], to_x), parts[2][half:]], axis=0)
    return swap(via_x, "dp", 1), swap(via_y, "dp", 2)


def finish(parts, got_x, got_y):
    return (parts[0].astype(F32) + got_x.astype(F32) + got_y.astype(F32)).astype(BF)


def collect_plain(grads_in, grads_out, z_parts, far_part):
    far_bit = lax.axis_size("mp") // 2
    sums = []
    for far in (0, 1):
        own, other = (jnp.stack([grads_in[2 * far + k], grads_out[2 * far + k]]) for k in range(2))
        sums.append(collect_dp(add_rounded(own, swap(other, "mp", 1))))
    count = lax.axis_size("mp") // 4
    stacked = jnp.concatenate([jnp.stack(jnp.split(part, count, axis=1)) for part in sums], axis=0)
    own = collect_z_relative(stacked)
    own = jnp.concatenate(
        [
            own.reshape(-1, own.shape[-1]),
            collect_z_relative(z_parts),
            add_rounded(far_part[0], swap(far_part[1], "mp", far_bit)),
        ],
        axis=0,
    )
    for bit in bits_of(lax.axis_size("dp")):
        own = jnp.concatenate([own, swap(own, "dp", bit)], axis=0)
    return own.reshape(lax.axis_size("dp"), -1, own.shape[-1])


def combine_everywhere(rows, combine, beside=None):
    step = 0
    for axis in ("dp", "mp"):
        for bit in bits_of(lax.axis_size(axis)):
            got = swap(rows, axis, bit)
            if beside is not None and step < len(beside):
                got, beside[step] = hold((got, beside[step]))
                step += 1
            rows = combine(rows, got)
    return rows


def ffn_forward(resid, gain_vec, shift_vec, blocks, b_out, beside=None):
    normed, unit_rows, inv_scale = norm_forward(resid, gain_vec, shift_vec)
    act = normed.astype(BF)
    branch = b_out
    uppers, hiddens = [], []
    for w_in_t, w_out, b_in in blocks:
        upper = dot_nt(act, w_in_t) + b_in
        hidden = jax.nn.silu(upper).astype(BF)
        branch = branch + dot_nn(hidden, w_out)
        uppers.append(upper)
        hiddens.append(hidden)
        if beside is not None and 2 * len(uppers) == len(blocks):
            branch, beside[0] = hold((branch, beside[0]))
    return branch, (unit_rows, inv_scale, act, uppers, hiddens)


def block_backward(grad_branch, act, block, upper, hidden):
    w_in_t, w_out, _ = block
    grad_hidden = dot_nt(grad_branch, w_out)
    grad_upper = (grad_hidden * swish_slope(upper)).astype(BF)
    return (
        dot_nn(grad_upper, w_in_t),
        dot_tn(grad_upper, act).astype(BF),
        dot_tn(hidden, grad_branch).astype(BF),
        jnp.sum(grad_upper, axis=0, dtype=F32, keepdims=True),
    )


def ffn_backward(grad_resid, saved, gain_vec, blocks, between=None):
    unit_rows, inv_scale, act, uppers, hiddens = saved
    grad_branch = (0.5 * grad_resid).astype(BF)
    grad_b_out = jnp.sum(grad_branch, axis=0, dtype=F32, keepdims=True)
    grad_act = 0.0
    count = len(blocks)
    grads_in, grads_out, grads_b = [None] * count, [None] * count, [None] * count
    for k in reversed(range(count)):
        part, grads_in[k], grads_out[k], grads_b[k] = block_backward(
            grad_branch, act, blocks[k], uppers[k], hiddens[k]
        )
        grad_act = grad_act + part
        if between is not None:
            grad_act, grad_branch, grads_in[k], grads_out[k] = between(
                k, (grad_act, grad_branch, grads_in[k], grads_out[k])
            )
    grad_in, grad_gain, grad_shift = norm_backward(grad_act, unit_rows, inv_scale, gain_vec)
    return (
        grad_resid + grad_in,
        (grads_in, grads_b, grads_out),
        (grad_gain, grad_shift, grad_b_out),
    )


def pair_mask(shape, head):
    lane = lax.broadcasted_iota(jnp.int32, shape, len(shape) - 1)
    return (lane // HEAD) == head


def attend_kernel(q_ref, k_ref, v_ref, bias_ref, out_ref, lse_ref):
    query, key, value = q_ref[...], k_ref[...], v_ref[...]
    bias = bias_ref[...]
    factor = LOG2E / math.sqrt(HEAD)
    mixed, logs = [], []
    for head in range(2):
        masked = jnp.where(pair_mask(query.shape, head), query, jnp.zeros_like(query))
        scores = dot_nt(masked, key) * factor + bias
        row_max = jnp.max(scores, axis=-1, keepdims=True)
        shifted = jnp.exp2(scores - row_max)
        total = jnp.sum(shifted, axis=-1, keepdims=True)
        probs = (shifted * (1.0 / total)).astype(BF)
        mixed.append(dot_nn(probs, value))
        logs.append(row_max + jnp.log2(total))
    first = pair_mask(mixed[0].shape, 0)
    out_ref[...] = jnp.where(first, mixed[0], mixed[1]).astype(BF)
    lse_ref[...] = jnp.where(first, logs[0], logs[1])


def attend_forward(query, key, value, bias, block):
    frames, columns = query.shape
    pairs = columns // (2 * HEAD)
    rows_spec = pl.BlockSpec((block, 2 * HEAD), lambda p, i: (i, p))
    whole_spec = pl.BlockSpec((frames, 2 * HEAD), lambda p, i: (0, p))
    return pl.pallas_call(
        attend_kernel,
        grid=(pairs, frames // block),
        in_specs=[rows_spec, whole_spec, whole_spec, pl.BlockSpec((1, frames), lambda p, i: (0, 0))],
        out_specs=[rows_spec, rows_spec],
        out_shape=[
            jax.ShapeDtypeStruct((frames, columns), BF),
            jax.ShapeDtypeStruct((frames, columns), F32),
        ],
        compiler_params=pltpu.CompilerParams(vmem_limit_bytes=48 * 1024 * 1024),
        cost_estimate=pl.CostEstimate(
            flops=8 * frames * frames * columns,
            bytes_accessed=12 * frames * columns,
            transcendentals=frames * frames * columns // HEAD,
        ),
        name="attend_forward",
    )(query, key, value, bias)


def attend_back_kernel(
    q_ref, k_ref, v_ref, g_ref, lse_ref, bias_ref, dq_ref, dk_ref, dv_ref, dk_acc, dv_acc
):
    step = pl.program_id(1)
    query, key, value, grad = q_ref[...], k_ref[...], v_ref[...], g_ref[...]
    bias = bias_ref[...]
    lse = lse_ref[...]
    factor = LOG2E / math.sqrt(HEAD)
    scale = 1.0 / math.sqrt(HEAD)
    dq, dk, dv = [], [], []
    for head in range(2):
        mask = pair_mask(query.shape, head)
        query_h = jnp.where(mask, query, jnp.zeros_like(query))
        grad_h = jnp.where(mask, grad, jnp.zeros_like(grad))
        scores = dot_nt(query_h, key) * factor + bias
        probs = jnp.exp2(scores - lse[:, head * HEAD : head * HEAD + 1])
        grad_probs = dot_nt(grad_h, value)
        row_dot = jnp.sum(probs * grad_probs, axis=-1, keepdims=True)
        grad_scores = (probs * (grad_probs - row_dot)).astype(BF)
        dv.append(dot_tn(probs.astype(BF), grad_h))
        dq.append(dot_nn(grad_scores, key))
        dk.append(dot_tn(grad_scores, query_h))
    first = pair_mask(dq[0].shape, 0)
    dq_ref[...] = (jnp.where(first, dq[0], dq[1]) * scale).astype(BF)
    new_dk = dk[0] + dk[1]
    new_dv = dv[0] + dv[1]

    @pl.when(step == 0)
    def _():
        dk_acc[...] = new_dk
        dv_acc[...] = new_dv

    @pl.when(step > 0)
    def _():
        dk_acc[...] += new_dk
        dv_acc[...] += new_dv

    @pl.when(step == pl.num_programs(1) - 1)
    def _():
        dk_ref[...] = (dk_acc[...] * scale).astype(BF)
        dv_ref[...] = dv_acc[...].astype(BF)


def attend_backward(query, key, value, grad, lse, bias, block):
    frames, columns = query.shape
    pairs = columns // (2 * HEAD)
    rows_spec = pl.BlockSpec((block, 2 * HEAD), lambda p, i: (i, p))
    whole_spec = pl.BlockSpec((frames, 2 * HEAD), lambda p, i: (0, p))
    shape = jax.ShapeDtypeStruct((frames, columns), BF)
    return pl.pallas_call(
        attend_back_kernel,
        grid=(pairs, frames // block),
        in_specs=[
            rows_spec,
            whole_spec,
            whole_spec,
            rows_spec,
            rows_spec,
            pl.BlockSpec((1, frames), lambda p, i: (0, 0)),
        ],
        out_specs=[rows_spec, whole_spec, whole_spec],
        out_shape=[shape, shape, shape],
        scratch_shapes=[
            pltpu.VMEM((frames, 2 * HEAD), F32),
            pltpu.VMEM((frames, 2 * HEAD), F32),
        ],
        compiler_params=pltpu.CompilerParams(vmem_limit_bytes=48 * 1024 * 1024),
        cost_estimate=pl.CostEstimate(
            flops=20 * frames * frames * columns,
            bytes_accessed=20 * frames * columns,
            transcendentals=frames * frames * columns // HEAD,
        ),
        name="attend_backward",
    )(query, key, value, grad, lse, bias)


def add_parts_kernel(one_ref, got_one_ref, two_ref, got_two_ref, out_ref):
    out_ref[0] = (one_ref[...].astype(F32) + got_one_ref[...].astype(F32)).astype(BF)
    out_ref[1] = (two_ref[...].astype(F32) + got_two_ref[...].astype(F32)).astype(BF)


def add_parts(one, got_one, two, got_two, parts):
    rows, width = one.shape
    part = rows // parts
    step = math.gcd(part, 256)
    steps = part // step
    spec = pl.BlockSpec((step, width), lambda p, j: (p * steps + j, 0))
    return pl.pallas_call(
        add_parts_kernel,
        grid=(parts, steps),
        in_specs=[spec] * 4,
        out_specs=pl.BlockSpec((None, 2, step, width), lambda p, j: (p, 0, j, 0)),
        out_shape=jax.ShapeDtypeStruct((parts, 2, part, width), BF),
        compiler_params=pltpu.CompilerParams(vmem_limit_bytes=32 * 1024 * 1024),
        cost_estimate=pl.CostEstimate(
            flops=2 * rows * width, bytes_accessed=12 * rows * width, transcendentals=0
        ),
        name="add_parts",
    )(one, got_one, two, got_two)


def unpack_kernel(index_ref, part_ref, in_ref, out_ref):
    rows = out_ref.shape[0]
    in_ref[...] = part_ref[:rows].astype(F32).T
    out_ref[...] = part_ref[rows:].astype(F32)


def unpack(parts, index, rows, place):
    count, _, width = parts.shape
    return pl.pallas_call(
        unpack_kernel,
        grid_spec=pltpu.PrefetchScalarGridSpec(
            num_scalar_prefetch=1,
            grid=(count,),
            in_specs=[
                pl.BlockSpec((None, 2 * rows, width), lambda r, at: (r, place // (2 * rows), 0))
            ],
            out_specs=[
                pl.BlockSpec((width, rows), lambda r, at: (0, at[0] ^ r)),
                pl.BlockSpec((rows, width), lambda r, at: (at[0] ^ r, 0)),
            ],
        ),
        out_shape=[
            jax.ShapeDtypeStruct((width, count * rows), F32),
            jax.ShapeDtypeStruct((count * rows, width), F32),
        ],
        compiler_params=pltpu.CompilerParams(vmem_limit_bytes=32 * 1024 * 1024),
        cost_estimate=pl.CostEstimate(
            flops=0, bytes_accessed=12 * count * rows * width, transcendentals=0
        ),
        name="unpack",
    )(index.reshape(1), parts)


def lay_out(buffer, before, rows, after, halo):
    count = rows.shape[0]
    buffer[:halo] = before[...]
    buffer[halo : halo + count] = rows[...]
    buffer[halo + count :] = after[...]


def depth_kernel(
    before_ref, rows_ref, after_ref, taps_ref, visible_ref, depth_ref, stats_ref, padded, *, taps
):
    count, lanes = depth_ref.shape
    halo = before_ref.shape[0]
    first = halo - taps // 2
    lay_out(padded, before_ref, rows_ref, after_ref, halo)
    depth = jnp.zeros((count, lanes), F32)
    for phase in range(8):
        more = (taps - 1 - phase) // 8
        base = padded[first + phase : first + phase + count + 8 * more]
        for step in range(more + 1):
            tap = 8 * step + phase
            depth = depth + base[8 * step : 8 * step + count] * taps_ref[tap : tap + 1]
    depth_ref[...] = depth
    visible = visible_ref[...]
    frames = jnp.sum(visible, axis=0, keepdims=True)
    mean = jnp.sum(depth * visible, axis=0, keepdims=True) / jnp.maximum(frames, 1.0)
    apart = (depth - mean) * visible
    stats_ref[0:1] = jnp.broadcast_to(frames, (1, lanes))
    stats_ref[1:2] = mean
    stats_ref[2:3] = jnp.sum(apart * apart, axis=0, keepdims=True)
    stats_ref[3:] = jnp.zeros((5, lanes), F32)


def depth_forward(rows, around, taps_rows, visible, taps):
    count, width = rows.shape
    lanes = 128
    halo = around[0].shape[0]

    def column(height):
        return pl.BlockSpec((height, lanes), lambda j: (0, j))

    return pl.pallas_call(
        functools.partial(depth_kernel, taps=taps),
        grid=(width // lanes,),
        in_specs=[
            column(halo),
            column(count),
            column(halo),
            column(taps_rows.shape[0]),
            pl.BlockSpec((count, 1), lambda j: (0, 0)),
        ],
        out_specs=[column(count), column(8)],
        out_shape=[
            jax.ShapeDtypeStruct((count, width), F32),
            jax.ShapeDtypeStruct((8, width), F32),
        ],
        scratch_shapes=[pltpu.VMEM((count + 2 * halo, lanes), F32)],
        cost_estimate=pl.CostEstimate(
            flops=2 * taps * count * width, bytes_accessed=9 * count * width, transcendentals=0
        ),
        name="depth_forward",
    )(around[0], rows, around[1], taps_rows, visible)


def depth_back_kernel(
    gbefore_ref,
    grad_ref,
    gafter_ref,
    before_ref,
    rows_ref,
    after_ref,
    taps_ref,
    visible_ref,
    value_ref,
    logistic_ref,
    gvalue_ref,
    ggate_ref,
    gtaps_ref,
    gbias_ref,
    gpadded,
    padded,
    *,
    taps,
):
    count, lanes = grad_ref.shape
    halo = before_ref.shape[0]
    first = halo - taps // 2
    lay_out(gpadded, gbefore_ref, grad_ref, gafter_ref, halo)
    lay_out(padded, before_ref, rows_ref, after_ref, halo)
    grad = grad_ref[...]
    total = jnp.zeros((count, lanes), F32)
    for phase in range(8):
        more = (taps - 1 - phase) // 8
        stop = first + phase + count + 8 * more
        gbase = gpadded[first + phase : stop]
        base = padded[first + phase : stop]
        for step in range(more + 1):
            tap = 8 * step + phase
            back = taps - 1 - tap
            total = total + gbase[8 * step : 8 * step + count] * taps_ref[back : back + 1]
            product = grad * base[8 * step : 8 * step + count]
            gtaps_ref[tap : tap + 1] = jnp.sum(product, axis=0, keepdims=True)
    grad_gated = total * visible_ref[...]
    logistic = logistic_ref[...]
    gvalue = (grad_gated * logistic).astype(BF)
    ggate = (grad_gated * value_ref[...] * logistic * (1.0 - logistic)).astype(BF)
    gvalue_ref[...] = gvalue
    ggate_ref[...] = ggate
    gbias_ref[0:1] = jnp.sum(gvalue.astype(F32), axis=0, keepdims=True)
    gbias_ref[1:2] = jnp.sum(ggate.astype(F32), axis=0, keepdims=True)
    gbias_ref[2:] = jnp.zeros((6, lanes), F32)


def depth_backward(grad, garound, rows, around, taps_rows, visible, value, logistic, taps):
    count, width = rows.shape
    lanes = 128
    halo = around[0].shape[0]

    def column(height):
        return pl.BlockSpec((height, lanes), lambda j: (0, j))

    return pl.pallas_call(
        functools.partial(depth_back_kernel, taps=taps),
        grid=(width // lanes,),
        in_specs=[
            column(halo),
            column(count),
            column(halo),
            column(halo),
            column(count),
            column(halo),
            column(taps_rows.shape[0]),
            pl.BlockSpec((count, 1), lambda j: (0, 0)),
            column(count),
            column(count),
        ],
        out_specs=[column(count), column(count), column(taps_rows.shape[0]), column(8)],
        out_shape=[
            jax.ShapeDtypeStruct((count, width), BF),
            jax.ShapeDtypeStruct((count, width), BF),
            jax.ShapeDtypeStruct(taps_rows.shape, F32),
            jax.ShapeDtypeStruct((8, width), F32),
        ],
        scratch_shapes=[pltpu.VMEM((count + 2 * halo, lanes), F32)] * 2,
        cost_estimate=pl.CostEstimate(
            flops=4 * taps * count * width, bytes_accessed=24 * count * width, transcendentals=0
        ),
        name="depth_backward",
    )(
        garound[0], grad, garound[1], around[0], rows, around[1], taps_rows, visible, value, logistic
    )


def spread_blocks(local, group):
    blocks = {0: local}
    for bit in reversed(bits_of(group)):
        for index in list(blocks):
            blocks[index | bit] = swap(blocks[index], "mp", bit)
    return [blocks[r] for r in range(group)]


def collect_blocks(parts):
    live = dict(enumerate(parts))
    for bit in bits_of(len(parts)):
        for index in [r for r in live if not r & bit]:
            sent = swap(live.pop(index | bit).astype(BF), "mp", bit)
            live[index] = live[index] + sent.astype(F32)
    return live[0]


def exchange_blocks(parts):
    return [parts[0]] + [swap(parts[r], "mp", r) for r in range(1, len(parts))]


def shards(
    frames,
    lengths,
    mask_flags,
    mask_embed,
    ffa_gain,
    ffa_shift,
    ffa_w_in,
    ffa_b_in,
    ffa_w_out,
    ffa_b_out,
    att_gain,
    att_shift,
    att_w_qkv,
    att_b_qv,
    att_w_out,
    att_b_out,
    conv_gain,
    conv_shift,
    conv_w_in,
    conv_b_in,
    conv_w_depth,
    batch_scale,
    batch_shift,
    running_mean,
    running_var,
    conv_w_out,
    conv_b_out,
    ffb_gain,
    ffb_shift,
    ffb_w_in,
    ffb_b_in,
    ffb_w_out,
    ffb_b_out,
    final_gain,
    final_shift,
    cotangent,
):
    mask_embed = mask_embed[None]
    ffa_gain = ffa_gain[None]
    ffa_shift = ffa_shift[None]
    ffa_b_out = ffa_b_out[None]
    att_gain = att_gain[None]
    att_shift = att_shift[None]
    att_b_out = att_b_out[None]
    conv_gain = conv_gain[None]
    conv_shift = conv_shift[None]
    conv_b_out = conv_b_out[None]
    ffb_gain = ffb_gain[None]
    ffb_shift = ffb_shift[None]
    ffb_b_out = ffb_b_out[None]
    final_gain = final_gain[None]
    final_shift = final_shift[None]
    dp = lax.axis_size("dp")
    mp = lax.axis_size("mp")
    zs = mp // 2
    group = mp // 2
    d = lax.axis_index("dp")
    m = lax.axis_index("mp")
    core = m % 2
    half = m // group
    q = m % group
    width = frames.shape[2]
    columns = width // mp
    rows_local = 2 * frames.shape[1]
    hidden_q = ffa_b_in.shape[0] // dp
    chan_q = columns // dp
    taps = conv_w_depth.shape[0]
    reach = taps // 2

    small = jnp.concatenate(
        [
            ffa_b_in.astype(F32).reshape(-1, columns),
            ffb_b_in.astype(F32).reshape(-1, columns),
            conv_b_in,
            conv_w_depth,
            batch_scale[None],
            batch_shift[None],
        ],
        axis=0,
    )
    per = ffa_b_in.shape[0] // columns
    low = mp // 4

    def relative_bias(far, near_core):
        first = far * (mp // 2) + near_core
        part = bias_rel[first : first + 2 * low : 2]
        return part.transpose(1, 0, 2).reshape(1, -1)


    def hidden_bias(rows):
        both = rows.reshape(zs, 2, dp * hidden_q).transpose(1, 0, 2).reshape(2, -1)
        own = lax.dynamic_slice_in_dim(both, core, 1, axis=0)
        other = lax.dynamic_slice_in_dim(both, 1 - core, 1, axis=0)
        return own, other

    def to_canon(rows):
        lead = rows.shape[:-1]
        split = rows.reshape(*lead, zs, 2, columns)
        return jnp.moveaxis(split, -3, -2).reshape(*lead, width)

    def from_canon(rows):
        lead = rows.shape[:-1]
        split = rows.reshape(*lead, 2, zs, columns)
        return jnp.moveaxis(split, -3, -2).reshape(*lead, width)

    def own_columns(rows):
        return lax.dynamic_slice_in_dim(rows, m * columns, columns, axis=-1)

    def hidden_pieces(w_in, w_out):
        piece_in = lax.dynamic_slice_in_dim(w_in, d * hidden_q, hidden_q, axis=1).T
        piece_out = lax.dynamic_slice_in_dim(w_out, d * hidden_q, hidden_q, axis=0)
        return piece_in, piece_out

    def channel_piece(rows):
        return lax.dynamic_slice_in_dim(rows, d * chan_q, chan_q, axis=0)

    kinds = [conv_w_in[0].T, conv_w_in[1].T, conv_w_out, att_w_out]
    valid_count = jnp.sum(lengths).astype(F32)
    for bit in bits_of(dp):
        valid_count = valid_count + swap(valid_count, "dp", bit)
    gathered, mid_z, late_z, halves, w_other, extras = spread_rounds(
        jnp.stack(hidden_pieces(ffa_w_in, ffa_w_out)),
        jnp.stack([channel_piece(rows) for rows in kinds]),
        jnp.stack(hidden_pieces(ffb_w_in, ffb_w_out)),
        split_halves(frames),
        att_w_qkv,
        (
            small[None],
            swap(att_b_qv, "mp", group),
            join_halves(*send_halves(*split_halves(mask_flags))),
            valid_count,
        ),
    )
    small, b_other, flag_rows, valid_count = extras
    bias_rel = small[:, :per].reshape(mp, dp, hidden_q)[:, jnp.arange(dp) ^ d]
    small = small[jnp.arange(mp) ^ m]
    bias_b = hidden_bias(small[:, per : 2 * per])
    conv_small = to_canon(jnp.moveaxis(small[:, 2 * per :], 0, 1).reshape(-1, width))
    rows_in = join_halves(*halves)
    flag_rows = flag_rows.astype(F32)[:, None]
    c_b_in = [conv_small[0:1], conv_small[1:2]]
    c_depth = jnp.pad(conv_small[2 : 2 + taps], ((0, -taps % 8), (0, 0)))
    c_scale = conv_small[2 + taps : 3 + taps]
    c_shift = conv_small[3 + taps : 4 + taps]
    blocks_a = [
        (gathered[k][0], gathered[k][1], relative_bias(k // 2, k % 2)) for k in range(4)
    ]
    mid_own = lax.all_gather(mid_z, "dp", axis=1, tiled=True)

    w_qkv = jnp.concatenate(
        [jnp.where(half == 0, att_w_qkv, w_other), jnp.where(half == 0, w_other, att_w_qkv)], axis=2
    )
    b_qv = jnp.concatenate(
        [jnp.where(half == 0, att_b_qv, b_other), jnp.where(half == 0, b_other, att_b_qv)], axis=1
    )


    length = lax.dynamic_index_in_dim(lengths, half, 0, keepdims=False)
    place = q * rows_local + jnp.arange(rows_local)
    visible = (place < length).astype(F32)[:, None]
    key_place = ((jnp.arange(group) ^ q)[:, None] * rows_local + jnp.arange(rows_local)).reshape(1, -1)
    key_bias = jnp.where(key_place < length, 0.0, -1e30).astype(F32)

    resid_a = rows_in.astype(F32) + flag_rows * mask_embed
    beside = [swap(late_z[0], "mp", 4)] if rounds_fit() else None
    branch, saved_a = ffn_forward(resid_a, ffa_gain, ffa_shift, blocks_a, ffa_b_out, beside)
    resid_b = resid_a + 0.5 * branch

    normed, att_unit, att_inv = norm_forward(resid_b, att_gain, att_shift)
    blocks = spread_blocks(normed.astype(BF), group)
    *blocks, mid_own, beside = hold((*blocks, mid_own, beside))
    if rounds_fit():
        far_near = swap(beside[0], "mp", 2)
    mid_other = swap(mid_own, "mp", 1)
    att_rows = jnp.concatenate(blocks, axis=0)
    query = (dot_nn(att_rows, w_qkv[0]) + b_qv[0]).astype(BF)
    key = dot_nn(att_rows, w_qkv[1]).astype(BF)
    value = (dot_nn(att_rows, w_qkv[2]) + b_qv[1]).astype(BF)
    if rounds_fit():
        query, key, value, far_near = hold((query, key, value, far_near))
        late_z = joined_z({0: late_z[0], 2: late_z[1], 4: beside[0], 6: far_near})
    late_own = lax.all_gather(late_z, "dp", axis=1, tiled=True)
    block = rows_local
    mixed_cols, lse = attend_forward(query, key, value, key_bias, block)
    parts = [mixed_cols[r * rows_local : (r + 1) * rows_local] for r in range(group)]
    parts = exchange_blocks(parts)
    mid = jnp.stack(
        [
            jnp.where(core == 0, one, two).reshape(4, zs, columns, width)
            for one, two in ((mid_own, mid_other), (mid_other, mid_own))
        ],
        axis=1,
    )
    conv_value_w, conv_gate_w, conv_out_w = (mid[k].reshape(width, width) for k in range(3))
    att_out_w = mid[3].transpose(1, 0, 2, 3).reshape(2, group, columns, width)
    att_out_w = reordered(jnp.moveaxis(att_out_w, 1, 0), q).reshape(width, width)
    *parts, conv_value_w, conv_gate_w, conv_out_w, att_out_w, cotangent = hold(
        (*parts, conv_value_w, conv_gate_w, conv_out_w, att_out_w, cotangent)
    )
    cot_halves = send_halves(*split_halves(cotangent))
    mixed = jnp.concatenate(parts, axis=1)
    resid_c = resid_b + (dot_nn(mixed, att_out_w) + att_b_out)

    normed, conv_unit, conv_inv = norm_forward(resid_c, conv_gain, conv_shift)
    conv_act = normed.astype(BF)
    pre_value = dot_nt(conv_act, conv_value_w) + c_b_in[0]
    pre_gate = dot_nt(conv_act, conv_gate_w) + c_b_in[1]
    logistic = jax.nn.sigmoid(pre_gate)
    gated = pre_value * logistic * visible

    up = [(i, i + 1) for i in range(mp - 1) if (i + 1) % group]
    down = [(i + 1, i) for i, _ in up]

    halo = -(-reach // 8) * 8

    def halos(rows):
        return lax.ppermute(rows[-halo:], "mp", up), lax.ppermute(rows[:halo], "mp", down)

    gated_halos = halos(gated)
    depth, stats = depth_forward(gated, gated_halos, c_depth, visible, taps)
    depth, stats, late_own, *cot_halves = hold((depth, stats, late_own, *cot_halves))
    cot_rows = join_halves(*cot_halves)
    late_own = late_own.reshape(2, -1, width)
    late_other = swap(late_own, "mp", 1)
    blocks_b = [(late_own[0], late_own[1], bias_b[0]), (late_other[0], late_other[1], bias_b[1])]

    def join(one, two):
        both = jnp.maximum(one[0:1] + two[0:1], 1.0)
        gap = one[1:2] - two[1:2]
        return jnp.concatenate(
            [
                one[0:1] + two[0:1],
                (one[0:1] * one[1:2] + two[0:1] * two[1:2]) / both,
                one[2:3] + two[2:3] + gap * gap * (one[0:1] * two[0:1] / both),
                one[3:],
            ],
            axis=0,
        )

    stats = combine_everywhere(stats, join)
    batch_mean = stats[1:2]
    batch_var = stats[2:3] / valid_count
    inv_batch = lax.rsqrt(batch_var + EPS)
    centred = depth - batch_mean
    normed_bn = centred * inv_batch * c_scale + c_shift
    swished = jax.nn.silu(normed_bn).astype(BF)
    resid_d = resid_c + (dot_nn(swished, conv_out_w) + conv_b_out)

    branch, saved_b = ffn_forward(resid_d, ffb_gain, ffb_shift, blocks_b, ffb_b_out)
    resid_e = resid_d + 0.5 * branch
    layer_rows, unit_out, inv_out = norm_forward(resid_e, final_gain, final_shift)

    grad_resid, g_final_gain, g_final_shift = norm_backward(
        cot_rows.astype(F32), unit_out, inv_out, final_gain
    )
    grad_resid, mats_b, vecs_b = ffn_backward(grad_resid, saved_b, ffb_gain, blocks_b)

    def by_core(rows):
        part = width // 2
        return [
            lax.dynamic_slice_in_dim(rows, which * part, part, axis=1) for which in (core, 1 - core)
        ]

    grad_branch = grad_resid.astype(BF)
    g_conv_b_out = jnp.sum(grad_branch, axis=0, dtype=F32, keepdims=True)
    grad_normed = dot_nt(grad_branch, conv_out_w) * swish_slope(normed_bn)
    g_conv_out = [dot_tn(rows, grad_branch).astype(BF) for rows in by_core(swished)]
    sums = jnp.concatenate(
        [
            jnp.sum(grad_normed, axis=0, keepdims=True),
            jnp.sum(grad_normed * centred, axis=0, keepdims=True),
        ],
        axis=0,
    )
    late_g = [mats_b[0][1], mats_b[2][1], mats_b[0][0], mats_b[2][0]]
    sums = combine_everywhere(sums, jnp.add, late_g)
    late_got = [swap(grads, "mp", 1) for grads in late_g[:2]]
    sums, layer_rows = hold((sums, layer_rows.astype(BF)))
    layer_out = send_back(layer_rows)
    grad_normed, *late_got = hold((grad_normed, *late_got))
    late_sum = add_parts(late_g[2], late_got[0], late_g[3], late_got[1], 1)
    late_sum = late_sum.reshape(2 * zs, dp * hidden_q, width)
    late_sum = lax.psum_scatter(late_sum, "dp", scatter_dimension=1, tiled=True)
    inv_cube = inv_batch * inv_batch * inv_batch
    grad_depth = grad_normed * (c_scale * inv_batch) - visible * (
        (inv_batch * c_scale * sums[0:1] + inv_cube * c_scale * sums[1:2] * centred) / valid_count
    )
    grad_value_pre, grad_gate_pre, g_depth, g_conv_b_in = depth_backward(
        grad_depth,
        halos(grad_depth),
        gated,
        gated_halos,
        c_depth,
        visible,
        pre_value,
        logistic,
        taps,
    )
    grad_act = dot_nn(grad_value_pre, conv_value_w) + dot_nn(grad_gate_pre, conv_gate_w)
    g_conv_value = [dot_tn(rows, conv_act).astype(BF) for rows in by_core(grad_value_pre)]
    g_conv_gate = [dot_tn(rows, conv_act).astype(BF) for rows in by_core(grad_gate_pre)]
    grad_in, g_conv_gain, g_conv_shift = norm_backward(grad_act, conv_unit, conv_inv, conv_gain)
    grad_resid = grad_resid + grad_in

    grad_branch = grad_resid.astype(BF)
    g_att_b_out = jnp.sum(grad_branch, axis=0, dtype=F32, keepdims=True)
    grad_mixed = dot_nt(grad_branch, att_out_w).astype(BF)
    g_att_out = []
    for which in range(2):
        one = [
            lax.dynamic_slice_in_dim(
                mixed,
                ((((q // 2) ^ k) * 2 + which) * 2 + slot) * columns,
                columns,
                axis=1,
            )
            for slot in range(2)
            for k in range(group // 2)
        ]
        g_att_out.append(dot_tn(jnp.concatenate(one, axis=1), grad_branch).astype(BF))
    wide = 2 * columns
    parts = [grad_mixed[:, r * wide : (r + 1) * wide] for r in range(group)]
    grad_cols = jnp.concatenate(exchange_blocks(parts), axis=0)
    grad_q, grad_k, grad_v = attend_backward(query, key, value, grad_cols, lse, key_bias, block // 2)

    mid_g = [g_conv_value, g_conv_gate, g_conv_out, g_att_out]
    mid_got = swap(jnp.concatenate([g[1] for g in mid_g], axis=0), "mp", 1)
    grad_all = jnp.concatenate([grad_q, grad_k, grad_v], axis=1)
    w_flat = jnp.concatenate([w_qkv[0], w_qkv[1], w_qkv[2]], axis=1)
    partial = dot_nt(grad_all, w_flat)
    g_qkv = dot_tn(grad_all, att_rows).astype(BF)
    partial, g_qkv, mid_got, *layer_out = hold((partial, g_qkv, mid_got, *layer_out))
    mid_got = mid_got.reshape(4, zs, columns, width)
    joint = [
        add_rounded(g[0].reshape(zs, columns, width), got)
        for g, got in zip(mid_g, mid_got, strict=True)
    ] + [g_qkv.reshape(6, columns, width)]
    joint_rows = (4 * zs + 6) * chan_q
    if rounds_fit():
        joint_parts = []
        for r in range(dp):
            part = [
                lax.dynamic_slice_in_dim(rows, (d ^ r) * chan_q, chan_q, axis=1) for rows in joint
            ]
            joint_parts.append(jnp.concatenate(part, axis=0).reshape(joint_rows, width))
        joint_corners = corners(joint_parts)
    grad_act = collect_blocks(
        [partial[r * rows_local : (r + 1) * rows_local] for r in range(group)]
    )
    if rounds_fit():
        grad_act, late_sum, *joint_corners = hold((grad_act, late_sum, *joint_corners))
        joint_sides = sides(joint_parts, *joint_corners)
    late_sum = late_sum.reshape(2, zs, hidden_q, width)
    late_parts = reordered(jnp.moveaxis(late_sum, 1, 0).reshape(zs, -1, width), m // 2)
    g_qv = jnp.stack(
        [jnp.sum(grad_q, axis=0, dtype=F32), jnp.sum(grad_v, axis=0, dtype=F32)]
    ).reshape(2, 2, 1, columns)
    g_b_qv = lax.dynamic_update_slice(
        jnp.zeros((2, 2, group, columns), F32), g_qv, (0, 0, q, 0)
    ).reshape(2, width)
    grad_in, g_att_gain, g_att_shift = norm_backward(grad_act, att_unit, att_inv, att_gain)
    grad_resid = grad_resid + grad_in

    def joint_pieces(rows):
        rows = rows.reshape(-1, chan_q, width)
        parts = jnp.moveaxis(rows[: 4 * zs].reshape(4, zs, chan_q, width), 1, 0)
        parts = reordered(parts.reshape(zs, -1, width), m // 2)
        pair = rows[4 * zs :].reshape(3, 2, chan_q, width)
        pair = [
            lax.dynamic_index_in_dim(pair, which, 1, keepdims=False).reshape(-1, width)
            for which in (half, 1 - half)
        ]
        return parts, pair

    flight = {}

    def between(k, held):
        if k == 3:
            held = hold(held)
            flight["b"] = [swap(held[2], "mp", 1), swap(held[3], "mp", 1)]
            flight["late"] = swap(late_parts[1::2], "mp", 2)
        elif k == 2:
            *held, b_in, b_out, side_x, side_y, late_got = hold(
                (*held, *flight["b"], *joint_sides, flight["late"])
            )
            parts = add_parts(held[2], b_in, held[3], b_out, 4)
            flight["b_parts"] = [parts[r].reshape(-1, width) for r in range(4)]
            flight["corners"] = corners(flight["b_parts"])
            late = add_rounded(late_parts[0::2], late_got)
            flight["late"] = [late[0], swap(late[1], "mp", 4)]
            flight["mid"], flight["pair"] = joint_pieces(finish(joint_parts, side_x, side_y))
        elif k == 1:
            mid = flight["mid"]
            *held, to_x, to_y, far = hold((*held, *flight["corners"], flight["late"][1]))
            flight["sides"] = sides(flight["b_parts"], to_x, to_y)
            flight["late"] = add_rounded(flight["late"][0], far)
            flight["a"] = [swap(held[2], "mp", 1), swap(held[3], "mp", 1)]
            flight["mid_got"] = swap(mid[1::2], "mp", 2)
        else:
            *held, a_in, a_out, mid_got = hold((*held, *flight["a"], flight["mid_got"]))
            parts = add_parts(held[2], a_in, held[3], a_out, 4)
            flight["a_parts"] = [parts[r].reshape(-1, width) for r in range(4)]
            flight["corners"] = corners(flight["a_parts"])
            mid = add_rounded(flight["mid"][0::2], mid_got)
            rows = jnp.concatenate([mid[1], flight["pair"][1]], axis=0)
            flight["far"] = [
                jnp.concatenate([mid[0], flight["pair"][0]], axis=0),
                swap(rows, "mp", 4),
            ]
        return held

    grad_resid, mats_a, vecs_a = ffn_backward(
        grad_resid, saved_a, ffa_gain, blocks_a, between if rounds_fit() else None
    )
    g_embed = jnp.sum(grad_resid * flag_rows, axis=0, keepdims=True)
    grad_frames = send_back(grad_resid.astype(BF))

    def hidden_order(parts):
        own, other = parts
        both = jnp.stack([jnp.where(core == 0, own, other), jnp.where(core == 0, other, own)])
        return both.reshape(2, zs, dp * hidden_q).transpose(1, 0, 2).reshape(-1, width)

    def relative_order(parts):
        rel = jnp.stack(parts).reshape(2, 2, dp, low, hidden_q)
        rel = rel.transpose(0, 3, 1, 2, 4).reshape(mp, dp, hidden_q)
        return rel[jnp.arange(mp) ^ m][:, jnp.arange(dp) ^ d].reshape(-1, width)

    small = (
        jnp.concatenate(
            [
                from_canon(jnp.concatenate([g_depth[:taps], g_conv_b_in[:2]], axis=0)),
                hidden_order(mats_b[1]),
                relative_order(mats_a[1]),
                g_b_qv,
                *vecs_b,
                g_final_gain,
                g_final_shift,
                g_conv_b_out,
                g_conv_gain,
                g_conv_shift,
                *vecs_a,
                g_embed,
                g_att_b_out,
                g_att_gain,
                g_att_shift,
            ],
            axis=0,
        )
    )
    if rounds_fit():
        b_x, b_y, *grad_frames, far, got = hold(
            (*flight["sides"], *grad_frames, flight["far"][1], swap(small, "dp", 1))
        )
        small = small + got
        b_sum = finish(flight["b_parts"], b_x, b_y).reshape(2, 2, hidden_q, width)
        rest = jnp.concatenate([flight["late"], add_rounded(flight["far"][0], far)], axis=0)
        to_x, to_y, b_near, got, rest = hold(
            (
                *flight["corners"],
                swap(b_sum[:, 1], "mp", 2),
                swap(small, "dp", 2),
                rest,
            )
        )
        small = small + got
        side_x, side_y = sides(flight["a_parts"], to_x, to_y)
        b_far, side_x, side_y, got, rest_x, rest_y = hold(
            (
                swap(add_rounded(b_sum[:, 0], b_near), "mp", 4),
                side_x,
                side_y,
                swap(small, "mp", 1),
                rest,
                rest,
            )
        )
        small = small + got
        a_sum = finish(flight["a_parts"], side_x, side_y).reshape(2, 2, hidden_q, width)
        a_near, got, rest_x, rest_y = hold(
            (
                swap(a_sum[:, 1], "mp", 2),
                swap(small, "mp", 2),
                swap(rest_x, "dp", 1),
                swap(rest_y, "dp", 2),
            )
        )
        small = small + got
        own = a_sum[:, 0].astype(F32) + a_near.astype(F32) + b_far.astype(F32)
        own = own.astype(BF).reshape(-1, width)
        cut = rest.shape[0] // 2
        by_x, by_y, got, rest_0, rest_1 = hold(
            (
                swap(own, "dp", 1),
                swap(own, "dp", 2),
                swap(small, "mp", 4),
                swap(rest_y[:cut], "dp", 1),
                swap(rest_x[cut:], "dp", 2),
            )
        )
        small = small + got
        corner = [swap(by_y[:hidden_q], "dp", 1), swap(by_x[hidden_q:], "dp", 2)]
        first = jnp.stack([own, by_x, by_y, jnp.concatenate(corner, axis=0)])
        rest = jnp.stack([rest, rest_x, rest_y, jnp.concatenate([rest_0, rest_1], axis=0)])
    else:
        joint = jnp.concatenate(joint, axis=0)
        joint = lax.psum_scatter(joint, "dp", scatter_dimension=1, tiled=True)
        mid_parts, pair = joint_pieces(joint)
        total = collect_plain(
            mats_a[0], mats_a[2], jnp.concatenate([late_parts, mid_parts], axis=1), pair
        )
        first, rest = total[:, : 2 * hidden_q], total[:, 2 * hidden_q :]
        small = combine_everywhere(small, jnp.add)
    if hidden_q % 128 == 0:
        g_ffa_in, g_ffa_out = unpack(first, d, hidden_q, 0)
        g_ffb_in, g_ffb_out = unpack(rest[:, : 2 * hidden_q], d, hidden_q, 0)
    else:
        pairs = []
        for part in (first, rest[:, : 2 * hidden_q]):
            part = reordered(part, d).reshape(dp, 2, hidden_q, width).astype(F32)
            part = jnp.moveaxis(part, 1, 0).reshape(2, -1, width)
            pairs += [part[0].T, part[1]]
        g_ffa_in, g_ffa_out, g_ffb_in, g_ffb_out = pairs
    rest = reordered(rest[:, 2 * hidden_q :], d).reshape(dp, 7, chan_q, width)
    rest = jnp.moveaxis(rest, 1, 0).reshape(7, columns, width).astype(F32)
    mid_total = rest[:4]
    g_att_qkv = rest[4:].transpose(0, 2, 1)

    total = small
    g_w_depth = own_columns(total[:taps])
    g_b_conv = own_columns(total[taps : taps + 2])
    at = taps + 2
    hidden_rows = mp * hidden_q * dp // width
    share = mats_b[1][0].shape[1] * 2 // mp

    def own_hidden(rows):
        return lax.dynamic_slice_in_dim(rows.reshape(-1), m * share, share, axis=0)

    g_ffb_b_in = own_hidden(total[at : at + hidden_rows])
    g_ffa_b_in = own_hidden(total[at + hidden_rows : at + 2 * hidden_rows])
    at = at + 2 * hidden_rows
    g_qv_out = own_columns(total[at : at + 2])
    e = total[at + 2 :]
    f = e[8:]

    def own_canon(vector):
        return own_columns(from_canon(vector))[0]

    mean_own = own_canon(batch_mean)
    var_own = own_canon(batch_var)
    g_scale = own_canon(sums[1:2] * inv_batch)
    g_shift = own_canon(sums[0:1])
    new_mean = 0.9 * running_mean + 0.1 * mean_own
    new_var = 0.9 * running_var + 0.1 * var_own * valid_count / (valid_count - 1.0)
    g_conv_w_in = jnp.stack([mid_total[0].T, mid_total[1].T])
    return (
        join_back(*layer_out),
        join_back(*grad_frames),
        f[3],
        f[0],
        f[1],
        g_ffa_in,
        g_ffa_b_in,
        g_ffa_out,
        f[2],
        f[5],
        f[6],
        g_att_qkv,
        g_qv_out,
        mid_total[3],
        f[4],
        e[6],
        e[7],
        g_conv_w_in,
        g_b_conv,
        g_w_depth,
        g_scale,
        g_shift,
        mid_total[2],
        e[5],
        e[0],
        e[1],
        g_ffb_in,
        g_ffb_b_in,
        g_ffb_out,
        e[2],
        e[3],
        e[4],
        new_mean,
        new_var,
    )


def solution(mesh):
    return jax.shard_map(
        shards,
        mesh=mesh,
        in_specs=(
            P("dp", "mp", None),
            P("dp"),
            P("dp", "mp"),
            P(),
            P(),
            P(),
            P(None, "mp"),
            P("mp"),
            P("mp", None),
            P(),
            P(),
            P(),
            P(None, None, "mp"),
            P(None, "mp"),
            P("mp", None),
            P(),
            P(),
            P(),
            P(None, None, "mp"),
            P(None, "mp"),
            P(None, "mp"),
            P("mp"),
            P("mp"),
            P("mp"),
            P("mp"),
            P("mp", None),
            P(),
            P(),
            P(),
            P(None, "mp"),
            P("mp"),
            P("mp", None),
            P(),
            P(),
            P(),
            P("dp", "mp", None),
        ),
        out_specs=(
            P("dp", "mp", None),
            P("dp", "mp", None),
            P(),
            P(),
            P(),
            P(None, "mp"),
            P("mp"),
            P("mp", None),
            P(),
            P(),
            P(),
            P(None, None, "mp"),
            P(None, "mp"),
            P("mp", None),
            P(),
            P(),
            P(),
            P(None, None, "mp"),
            P(None, "mp"),
            P(None, "mp"),
            P("mp"),
            P("mp"),
            P("mp", None),
            P(),
            P(),
            P(),
            P(None, "mp"),
            P("mp"),
            P("mp", None),
            P(),
            P(),
            P(),
            P("mp"),
            P("mp"),
        ),
        check_vma=False,
    )
```

time: 2490 us -> 851 us (0.34)
  waiting for transfers between devices: 1820 us -> 282 us
  matrix products: 306 us -> 126 us
  blocking collectives: 140 us -> 0 us
  starting transfers between devices: 0.69 us -> 133 us
  Pallas kernels: 0 us -> 113 us
  other arithmetic: 123 us -> 84.9 us
    reduce_scatter x8 -> x1, waiting for transfers between devices: 1120 us -> 0.01 us  [shards(): late_sum = lax.psum_scatter(late_sum, 'dp', scatter_dimension=1, tiled=True)]
    all_gather x8 -> x2, waiting for transfers between devices: 561 us -> 17.5 us  [the longest x1 17.5 us: shards(): late_own = lax.all_gather(late_z, 'dp', axis=1, tiled=True)]
    ppermute x0 -> x103, waiting for transfers between devices: none -> 265 us  [the longest x89 251 us: swap(): return lax.ppermute(values, axis, [(i, i ^ bit) for i in range(count)])]
    dot_general x38 -> x57, matrix products: 306 us -> 126 us  [the longest x17 43.7 us: dot_nt(): lax.dot_general(left, right, (((1,), (1,)), ((), ())), preferred_element_...]
    psum x1 -> x0, waiting for transfers between devices: 137 us -> none  [shards(): lax.psum((ffa_mats[0], ffa_mats[1], ffa_mats[2], att_mats[0], att_mats[1]...]
    ppermute x0 -> x103, starting transfers between devices: none -> 133 us  [the longest x89 106 us: swap(): return lax.ppermute(values, axis, [(i, i ^ bit) for i in range(count)])]
    pallas_call x0 -> x9, Pallas kernels: none -> 113 us  [the longest x1 49.2 us: attend_backward(): pl.pallas_call(attend_back_kernel, grid=(pairs, frames // block), in_spec...]
    psum x5 -> x0, blocking collectives: 86.4 us -> none  [the longest x1 39.4 us: shards(): lax.psum((grad_embed, ffa_vecs[0], ffa_vecs[1], ffa_vecs[2], att_vecs[0],...]
  transfers between devices with their start and end apart: 17 -> 106, of which waited for: 17 -> 49; matrix products, arithmetic and copies ran while one was open for 5% -> 23% of each run, Pallas kernels for 0% -> 12%
where the time goes in v1:
time: 851 us; the launch traced here: 842 us
  waiting for transfers between devices  282 us (33%)
  starting transfers between devices  133 us (16%)
  matrix products  126 us (15%)
  Pallas kernels  113 us (13%)
  other arithmetic  84.9 us (10%)
  local copies, waits for them, and re-layouts  82.9 us (10%)
  between operations  19.8 us (2%)
    ppermute x89, waiting for transfers between devices, swap(): return lax.ppermute(values, axis, [(i, i ^ bit) for i in range(count)])  251 us
    ppermute x89, starting transfers between devices, swap(): return lax.ppermute(values, axis, [(i, i ^ bit) for i in range(count)])  106 us
    pallas_call x1, Pallas kernels, attend_backward(): pl.pallas_call(attend_back_kernel, grid=(pairs, frames // block), in_spec...  49.2 us
    dot_general x17, matrix products, dot_nt(): lax.dot_general(left, right, (((1,), (1,)), ((), ())), preferred_element_...  43.7 us
    unnamed x419, local copies, waits for them, and re-layouts  43.7 us
    dot_general x19, matrix products, dot_nn(): lax.dot_general(left, right, (((1,), (0,)), ((), ())), preferred_element_...  41.1 us
    dot_general x21, matrix products, dot_tn(): lax.dot_general(left, right, (((0,), (0,)), ((), ())), preferred_element_...  40.8 us
    pallas_call x1, Pallas kernels, attend_forward(): pl.pallas_call(attend_kernel, grid=(pairs, frames // block), in_specs=[ro...  28.5 us
  transfers between devices with their start and end apart: 106, of which 49 were waited for; matrix products, arithmetic and copies ran while one was open for 23% of the time, Pallas kernels for 12%

profile of v1, /device:TPU:0, one launch (start us, length us, event | category | flops | bytes accessed | tf_op | source)
XLA Modules:
  0.0 842.0 jit_solution(4077620674108337336)
XLA Ops:
  31.9 6.4 collective-permute-start.3
  53.5 12.3 %collective-permute-done.13 = f32[2,43,128]{2,0,1:T(2,128)S(1)} collective-permute-done((f32[2,43,128]{2,0,1:T(2,128)S(1)}, f32[2,43,128]{2,0,1:T(2,128)S(1)}, u32[]{:S(2)}, u32[]{:S(2)}) %collective-permute-start.13) | collective-permute-done | bytes 44064 | tf_op jit(solution)/shard_map/ppermute | solution.py:32
  83.6 6.8 collective-permute-done.21
  101.8 6.5 collective-permute-done.17
  108.3 9.2 %collective-permute-done.19 = bf16[2,128,1024]{2,1,0:T(8,128)(2,1)S(1)} collective-permute-done((bf16[2,128,1024]{2,1,0:T(8,128)(2,1)S(1)}, bf16[2,128,1024]{2,1,0:T(8,128)(2,1)S(1)}, u32[]{:S(2)}, u32[]{:S(2)}) %collective-permute-start.19) | collective-permute-done | bytes 524320 | tf_op jit(solution)/shard_map/ppermute | solution.py:32
  138.4 8.5 %collective-permute-start.27 = (bf16[2,128,1024]{2,1,0:T(8,128)(2,1)S(1)}, bf16[2,128,1024]{2,1,0:T(8,128)(2,1)S(1)}, u32[]{:S(2)}, u32[]{:S(2)}) collective-permute-start(bf16[2,128,1024]{2,1,0:T(8,128)(2,1)S(1)} %copy-done.47), channel_id=1, source_target_pairs={{0,4},{1,5},{2,6},{3,7},{4,0},{5,1},{6,2},{7,3},{8,12},{9,13},{10,... | collective-permute-start | bytes 1572872 | tf_op jit(solution)/shard_map/ppermute | solution.py:32
  162.0 8.2 collective-permute-done.27
  179.2 19.7 %collective-permute-done.30 = bf16[416,1024]{1,0:T(8,128)(2,1)S(1)} collective-permute-done((bf16[416,1024]{1,0:T(8,128)(2,1)S(1)}, bf16[416,1024]{1,0:T(8,128)(2,1)S(1)}, u32[]{:S(2)}, u32[]{:S(2)}) %collective-permute-start.30) | collective-permute-done | bytes 852000 | tf_op jit(solution)/shard_map/ppermute | solution.py:32
  208.4 7.9 collective-permute-done.32
  222.1 28.5 %attend_forward.1 = (bf16[1664,256]{1,0:T(8,128)(2,1)S(1)}, f32[1664,256]{1,0:T(8,128)S(1)}) custom-call(bf16[1664,256]{1,0:T(8,128)(2,1)S(1)} %fusion.6.q_ref, bf16[1664,256]{1,0:T(8,128)(2,1)S(1)} %convolution_convert_fusion.4.k_ref, bf16[1664,256]{1,0:T(8,128)(2,1)S(1)} %fusion.7.v_ref, f32[1,1664]{1,0:T(1,128)S(1)} %select_n.398.bias_ref), custom_call_target="tpu_custom_call" | custom-call | flops 5670699008 | bytes 5111808 | tf_op jit(solution)/shard_map/attend_forward/pallas_call | solution.py:392
  283.1 7.7 depth_forward.1
  290.9 17.5 %all-gather.5.cloned.1.call-done = bf16[8,512,1024]{2,1,0:T(8,128)(2,1)} async-done(((bf16[8,128,1024]{2,1,0:T(8,128)(2,1)}), bf16[8,512,1024]{2,1,0:T(8,128)(2,1)}) %all-gather.5.cloned.1.call-update) | async-done | bytes 8388624 | tf_op jit(solution)/shard_map/all_gather | solution.py:900
  385.9 10.1 %collective-permute-done.51 = f32[2,1024]{1,0:T(2,128)S(1)} collective-permute-done((f32[2,1024]{1,0:T(2,128)S(1)}, f32[2,1024]{1,0:T(2,128)S(1)}, u32[]{:S(2)}, u32[]{:S(2)}) %collective-permute-start.51) | collective-permute-done | bytes 8224 | tf_op jit(solution)/shard_map/ppermute | solution.py:32
  423.8 14.8 %depth_backward.1 = (bf16[416,1024]{1,0:T(8,128)(2,1)}, bf16[416,1024]{1,0:T(8,128)(2,1)}, f32[32,1024]{1,0:T(8,128)}, f32[8,1024]{1,0:T(8,128)}) custom-call(f32[16,1024]{1,0:T(8,128)} %copy-done.108, f32[416,1024]{1,0:T(8,128)} %copy-done.24, f32[16,1024]{1,0:T(8,128)} %copy-done.109, f32[16,1024]{1,0:T(8,128)} %copy-done.91, f32[416,1024]{1,0:T(8,128)} %copy-done.12, ...), custom_call_target="tpu_custom_call" | custom-call | flops 52822016 | bytes 10223616 | tf_op jit(solution)/shard_map/depth_backward/pallas_call | solution.py:665
  465.9 7.1 collective-permute-done.57
  474.3 49.2 %attend_backward.1 = (bf16[1664,256]{1,0:T(8,128)(2,1)S(1)}, bf16[1664,256]{1,0:T(8,128)(2,1)S(1)}, bf16[1664,256]{1,0:T(8,128)(2,1)S(1)}) custom-call(bf16[1664,256]{1,0:T(8,128)(2,1)S(1)} %fusion.6.q_ref, bf16[1664,256]{1,0:T(8,128)(2,1)S(1)} %convolution_convert_fusion.4.k_ref, bf16[1664,256]{1,0:T(8,128)(2,1)S(1)} %fusion.7.v_ref, ...), custom_call_target="tpu_custom_call" | custom-call | flops 14176747520 | bytes 8519680 | tf_op jit(solution)/shard_map/attend_backward/pallas_call | solution.py:460
  553.1 13.7 %collective-permute-done.64 = bf16[416,1024]{1,0:T(8,128)(2,1)S(1)} collective-permute-done((bf16[416,1024]{1,0:T(8,128)(2,1)S(1)}, bf16[416,1024]{1,0:T(8,128)(2,1)S(1)}, u32[]{:S(2)}, u32[]{:S(2)}) %collective-permute-start.64) | collective-permute-done | bytes 852000 | tf_op jit(solution)/shard_map/ppermute | solution.py:32
  597.7 20.0 %collective-permute-done.71 = bf16[2,256,1024]{2,1,0:T(8,128)(2,1)S(1)} collective-permute-done((bf16[2,256,1024]{2,1,0:T(8,128)(2,1)S(1)}, bf16[2,256,1024]{2,1,0:T(8,128)(2,1)S(1)}, u32[]{:S(2)}, u32[]{:S(2)}) %collective-permute-start.71) | collective-permute-done | bytes 1048608 | tf_op jit(solution)/shard_map/ppermute | solution.py:32
  644.9 13.8 %collective-permute-done.74 = bf16[256,1024]{1,0:T(8,128)(2,1)S(1)} collective-permute-done((bf16[256,1024]{1,0:T(8,128)(2,1)S(1)}, bf16[256,1024]{1,0:T(8,128)(2,1)S(1)}, u32[]{:S(2)}, u32[]{:S(2)}) %collective-permute-start.74) | collective-permute-done | bytes 524320 | tf_op jit(solution)/shard_map/ppermute | solution.py:32
  696.3 7.0 collective-permute-done.83
  710.3 8.2 collective-permute-done.82
  741.4 21.1 %collective-permute-done.88 = bf16[2,128,1024]{2,1,0:T(8,128)(2,1)} collective-permute-done((bf16[2,128,1024]{2,1,0:T(8,128)(2,1)}, bf16[2,128,1024]{2,1,0:T(8,128)(2,1)}, u32[]{:S(2)}, u32[]{:S(2)}) %collective-permute-start.88) | collective-permute-done | bytes 524320 | tf_op jit(solution)/shard_map/ppermute | solution.py:32
  771.7 14.0 %collective-permute-done.93 = f32[58,1024]{1,0:T(8,128)S(1)} collective-permute-done((f32[58,1024]{1,0:T(8,128)S(1)}, f32[58,1024]{1,0:T(8,128)S(1)}, u32[]{:S(2)}, u32[]{:S(2)}) %collective-permute-start.93) | collective-permute-done | bytes 237600 | tf_op jit(solution)/shard_map/ppermute | solution.py:32
  796.6 8.8 %collective-permute-done.98 = f32[58,1024]{1,0:T(8,128)S(1)} collective-permute-done((f32[58,1024]{1,0:T(8,128)S(1)}, f32[58,1024]{1,0:T(8,128)S(1)}, u32[]{:S(2)}, u32[]{:S(2)}) %collective-permute-start.98) | collective-permute-done | bytes 237600 | tf_op jit(solution)/shard_map/ppermute | solution.py:32
  (943 shorter events, 495.2 us)
Async XLA Ops:
  7.3 194.4 %all-gather.3.cloned.1.call-start = ((), (), s32[]{:S(2)}) async-start(), calls=%async_computation.1 | async-start | bytes 5242880 | tf_op jit(solution)/shard_map/all_gather | solution.py:866
  10.5 29.3 %collective-permute-start = (bf16[2,128,1024]{2,1,0:T(8,128)(2,1)S(1)}, bf16[2,128,1024]{2,1,0:T(8,128)(2,1)S(1)}, u32[]{:S(2)}, u32[]{:S(2)}) collective-permute-start(bf16[2,128,1024]{2,1,0:T(8,128)(2,1)S(1)} %get-tuple-element.563), channel_id=1, source_target_pairs={{0,2},{1,3},{2,0},{3,1},{4,6},{5,7},{6,4},{7,5},{8,10},{9,11},{10,... | collective-permute-start | bytes 1572872 | tf_op jit(solution)/shard_map/ppermute | solution.py:32
  41.8 32.9 %collective-permute-start.8 = (bf16[2,256,1024]{2,1,0:T(8,128)(2,1)}, bf16[2,256,1024]{2,1,0:T(8,128)(2,1)S(1)}, u32[]{:S(2)}, u32[]{:S(2)}) collective-permute-start(bf16[2,256,1024]{2,1,0:T(8,128)(2,1)} %pad_maximum_fusion.13), channel_id=1, source_target_pairs={{0,8},{8,0},{16,24},{24,16},{1,9},{9,1},{17,25},{25,17},{2,10},{10... | collective-permute-start | bytes 3145736 | tf_op jit(solution)/shard_map/ppermute | solution.py:32
  43.3 31.4 %collective-permute-start.9 = (bf16[2,256,1024]{2,1,0:T(8,128)(2,1)}, bf16[2,256,1024]{2,1,0:T(8,128)(2,1)S(1)}, u32[]{:S(2)}, u32[]{:S(2)}) collective-permute-start(bf16[2,256,1024]{2,1,0:T(8,128)(2,1)} %pad_maximum_fusion.13), channel_id=1, source_target_pairs={{0,16},{8,24},{16,0},{24,8},{1,17},{9,25},{17,1},{25,9},{2,18},{10... | collective-permute-start | bytes 3145736 | tf_op jit(solution)/shard_map/ppermute | solution.py:32
  44.8 29.9 %collective-permute-start.10 = (bf16[2,128,1024]{2,1,0:T(8,128)(2,1)}, bf16[2,128,1024]{2,1,0:T(8,128)(2,1)}, u32[]{:S(2)}, u32[]{:S(2)}) collective-permute-start(bf16[2,128,1024]{2,1,0:T(8,128)(2,1)} %copy-done.76), channel_id=1, source_target_pairs={{0,2},{1,3},{2,0},{3,1},{4,6},{5,7},{6,4},{7,5},{8,10},{9,11},{10,... | collective-permute-start | bytes 1572872 | tf_op jit(solution)/shard_map/ppermute | solution.py:32
  77.3 40.2 %collective-permute-start.14 = (bf16[2,256,1024]{2,1,0:T(8,128)(2,1)S(1)}, bf16[2,256,1024]{2,1,0:T(8,128)(2,1)S(1)}, u32[]{:S(2)}, u32[]{:S(2)}) collective-permute-start(bf16[2,256,1024]{2,1,0:T(8,128)(2,1)S(1)} %get-tuple-element.558), channel_id=1, source_target_pairs={{0,8},{8,0},{16,24},{24,16},{1,9},{9,1},{17,25},{25,17},{2,10},{10... | collective-permute-start | bytes 3145736 | tf_op jit(solution)/shard_map/ppermute | solution.py:32
  78.9 38.6 %collective-permute-start.15 = (bf16[2,256,1024]{2,1,0:T(8,128)(2,1)S(1)}, bf16[2,256,1024]{2,1,0:T(8,128)(2,1)S(1)}, u32[]{:S(2)}, u32[]{:S(2)}) collective-permute-start(bf16[2,256,1024]{2,1,0:T(8,128)(2,1)S(1)} %get-tuple-element.558), channel_id=1, source_target_pairs={{0,16},{8,24},{16,0},{24,8},{1,17},{9,25},{17,1},{25,9},{2,18},{10... | collective-permute-start | bytes 3145736 | tf_op jit(solution)/shard_map/ppermute | solution.py:32
  135.8 34.5 %collective-permute-start.28 = (bf16[2,1024,1024]{2,1,0:T(8,128)(2,1)}, bf16[2,1024,1024]{2,1,0:T(8,128)(2,1)}, u32[]{:S(2)}, u32[]{:S(2)}) collective-permute-start(bf16[2,1024,1024]{2,1,0:T(8,128)(2,1)} %maximum_dynamic-update-slice_fusion.1), channel_id=1, source_target_pairs={{0,1},{1,0},{2,3},{3,2},{4,5},{5,4},{6,7},{7,6},{8,9},{9,8},{10,11... | collective-permute-start | bytes 12582920 | tf_op jit(solution)/shard_map/ppermute | solution.py:32
  138.2 170.2 %all-gather.5.cloned.1.call-start = ((), (), s32[]{:S(2)}) async-start(), calls=%async_computation.2 | async-start | bytes 10485760 | tf_op jit(solution)/shard_map/all_gather | solution.py:900
  138.4 31.8 %collective-permute-start.27 = (bf16[2,128,1024]{2,1,0:T(8,128)(2,1)S(1)}, bf16[2,128,1024]{2,1,0:T(8,128)(2,1)S(1)}, u32[]{:S(2)}, u32[]{:S(2)}) collective-permute-start(bf16[2,128,1024]{2,1,0:T(8,128)(2,1)S(1)} %copy-done.47), channel_id=1, source_target_pairs={{0,4},{1,5},{2,6},{3,7},{4,0},{5,1},{6,2},{7,3},{8,12},{9,13},{10,... | collective-permute-start | bytes 1572872 | tf_op jit(solution)/shard_map/ppermute | solution.py:32
  218.5 349.9 %reduce-scatter.2.cloned.1.call-start = ((), (), s32[]{:S(2)}) async-start(), calls=%async_computation.3 | async-start | bytes 10485760 | tf_op jit(solution)/shard_map/reduce_scatter | solution.py:1001
  218.6 34.0 %collective-permute-start.36 = (bf16[16,128,1024]{2,1,0:T(8,128)(2,1)}, bf16[16,128,1024]{2,1,0:T(8,128)(2,1)}, u32[]{:S(2)}, u32[]{:S(2)}) collective-permute-start(bf16[16,128,1024]{2,1,0:T(8,128)(2,1)} %all-gather.3.cloned.1.call-done), channel_id=1, source_target_pairs={{0,1},{1,0},{2,3},{3,2},{4,5},{5,4},{6,7},{7,6},{8,9},{9,8},{10,11... | collective-permute-start | bytes 12582920 | tf_op jit(solution)/shard_map/ppermute | solution.py:32
  308.4 31.3 %collective-permute-start.46 = (bf16[2,2048,1024]{2,1,0:T(8,128)(2,1)}, bf16[2,2048,1024]{2,1,0:T(8,128)(2,1)}, u32[]{:S(2)}, u32[]{:S(2)}) collective-permute-start(bf16[2,2048,1024]{2,1,0:T(8,128)(2,1)} %bitcast.520), channel_id=1, source_target_pairs={{0,1},{1,0},{2,3},{3,2},{4,5},{5,4},{6,7},{7,6},{8,9},{9,8},{10,11... | collective-permute-start | bytes 25165832 | tf_op jit(solution)/shard_map/ppermute | solution.py:32
  452.8 79.0 %collective-permute-start.59 = (bf16[2048,1024]{1,0:T(8,128)(2,1)}, bf16[2048,1024]{1,0:T(8,128)(2,1)}, u32[]{:S(2)}, u32[]{:S(2)}) collective-permute-start(bf16[2048,1024]{1,0:T(8,128)(2,1)} %pad_maximum_fusion), channel_id=1, source_target_pairs={{0,1},{1,0},{2,3},{3,2},{4,5},{5,4},{6,7},{7,6},{8,9},{9,8},{10,11... | collective-permute-start | bytes 12582920 | tf_op jit(solution)/shard_map/ppermute | solution.py:32
  460.7 71.0 %collective-permute-start.60 = (bf16[208,1024]{1,0:T(8,128)(2,1)}, bf16[208,1024]{1,0:T(8,128)(2,1)S(1)}, u32[]{:S(2)}, u32[]{:S(2)}) collective-permute-start(bf16[208,1024]{1,0:T(8,128)(2,1)} %get-tuple-element.538), channel_id=1, source_target_pairs={{0,0},{4,1},{1,2},{5,3},{2,4},{6,5},{3,6},{7,7},{8,8},{12,9},{9,10... | collective-permute-start | bytes 1277960 | tf_op jit(solution)/shard_map/ppermute | solution.py:97
  465.3 66.4 %collective-permute-start.61 = (bf16[208,1024]{1,0:T(8,128)(2,1)}, bf16[208,1024]{1,0:T(8,128)(2,1)S(1)}, u32[]{:S(2)}, u32[]{:S(2)}) collective-permute-start(bf16[208,1024]{1,0:T(8,128)(2,1)} %get-tuple-element.537), channel_id=1, source_target_pairs={{4,0},{0,1},{5,2},{1,3},{6,4},{2,5},{7,6},{3,7},{12,8},{8,9},{13,1... | collective-permute-start | bytes 1277960 | tf_op jit(solution)/shard_map/ppermute | solution.py:98
  582.1 38.4 %collective-permute-start.67 = (bf16[1024,1024]{1,0:T(8,128)(2,1)S(1)}, bf16[1024,1024]{1,0:T(8,128)(2,1)S(1)}, u32[]{:S(2)}, u32[]{:S(2)}) collective-permute-start(bf16[1024,1024]{1,0:T(8,128)(2,1)S(1)} %convolution_convert_fusion.12), channel_id=1, source_target_pairs={{0,1},{1,0},{2,3},{3,2},{4,5},{5,4},{6,7},{7,6},{8,9},{9,8},{10,11... | collective-permute-start | bytes 6291464 | tf_op jit(solution)/shard_map/ppermute | solution.py:32
  582.2 38.3 %collective-permute-start.68 = (bf16[1024,1024]{1,0:T(8,128)(2,1)S(1)}, bf16[1024,1024]{1,0:T(8,128)(2,1)S(1)}, u32[]{:S(2)}, u32[]{:S(2)}) collective-permute-start(bf16[1024,1024]{1,0:T(8,128)(2,1)S(1)} %convolution_convert_fusion.11), channel_id=1, source_target_pairs={{0,1},{1,0},{2,3},{3,2},{4,5},{5,4},{6,7},{7,6},{8,9},{9,8},{10,11... | collective-permute-start | bytes 6291464 | tf_op jit(solution)/shard_map/ppermute | solution.py:32
  584.2 33.6 %collective-permute-start.69 = (bf16[704,1024]{1,0:T(8,128)(2,1)S(1)}, bf16[704,1024]{1,0:T(8,128)(2,1)S(1)}, u32[]{:S(2)}, u32[]{:S(2)}) collective-permute-start(bf16[704,1024]{1,0:T(8,128)(2,1)S(1)} %pad_maximum_fusion.11), channel_id=1, source_target_pairs={{0,8},{8,0},{16,24},{24,16},{1,9},{9,1},{17,25},{25,17},{2,10},{10... | collective-permute-start | bytes 4325384 | tf_op jit(solution)/shard_map/ppermute | solution.py:32
  586.9 33.6 %collective-permute-start.70 = (bf16[704,1024]{1,0:T(8,128)(2,1)S(1)}, bf16[704,1024]{1,0:T(8,128)(2,1)S(1)}, u32[]{:S(2)}, u32[]{:S(2)}) collective-permute-start(bf16[704,1024]{1,0:T(8,128)(2,1)S(1)} %pad_maximum_fusion.12), channel_id=1, source_target_pairs={{0,16},{8,24},{16,0},{24,8},{1,17},{9,25},{17,1},{25,9},{2,18},{10... | collective-permute-start | bytes 4325384 | tf_op jit(solution)/shard_map/ppermute | solution.py:32
  636.6 35.4 %collective-permute-start.79 = (bf16[2,128,1024]{2,1,0:T(8,128)(2,1)S(1)}, bf16[2,128,1024]{2,1,0:T(8,128)(2,1)S(1)}, u32[]{:S(2)}, u32[]{:S(2)}) collective-permute-start(bf16[2,128,1024]{2,1,0:T(8,128)(2,1)S(1)} %slice.688), channel_id=1, source_target_pairs={{0,2},{1,3},{2,0},{3,1},{4,6},{5,7},{6,4},{7,5},{8,10},{9,11},{10,... | collective-permute-start | bytes 1572872 | tf_op jit(solution)/shard_map/ppermute | solution.py:32
  660.7 33.3 %collective-permute-start.75 = (bf16[512,1024]{1,0:T(8,128)(2,1)}, bf16[512,1024]{1,0:T(8,128)(2,1)}, u32[]{:S(2)}, u32[]{:S(2)}) collective-permute-start(bf16[512,1024]{1,0:T(8,128)(2,1)} %pad_maximum_fusion.15), channel_id=1, source_target_pairs={{0,8},{8,0},{16,24},{24,16},{1,9},{9,1},{17,25},{25,17},{2,10},{10... | collective-permute-start | bytes 3145736 | tf_op jit(solution)/shard_map/ppermute | solution.py:32
  681.2 29.0 %collective-permute-start.81 = (bf16[208,1024]{1,0:T(8,128)(2,1)}, bf16[208,1024]{1,0:T(8,128)(2,1)}, u32[]{:S(2)}, u32[]{:S(2)}) collective-permute-start(bf16[208,1024]{1,0:T(8,128)(2,1)} %get-tuple-element.525), channel_id=1, source_target_pairs={{4,0},{0,1},{5,2},{1,3},{6,4},{2,5},{7,6},{3,7},{12,8},{8,9},{13,1... | collective-permute-start | bytes 1277960 | tf_op jit(solution)/shard_map/ppermute | solution.py:98
  683.1 35.4 %collective-permute-start.82 = (bf16[224,1024]{1,0:T(8,128)(2,1)}, bf16[224,1024]{1,0:T(8,128)(2,1)}, u32[]{:S(2)}, u32[]{:S(2)}) collective-permute-start(bf16[224,1024]{1,0:T(8,128)(2,1)} %pad_maximum_fusion.40), channel_id=1, source_target_pairs={{0,4},{1,5},{2,6},{3,7},{4,0},{5,1},{6,2},{7,3},{8,12},{9,13},{10,... | collective-permute-start | bytes 1376264 | tf_op jit(solution)/shard_map/ppermute | solution.py:32
  (282 other events, 2823.8 us)
Sparse Core Ops, SparseCore 0:
  138.3 60.3 all-gather.2
  218.7 89.6 all-gather.4
  405.4 85.4 reduce-scatter.1

commit v2 on v1

--- a/solution.py
+++ b/solution.py
@@ -85,18 +85,32 @@
     return jnp.concatenate([lower, upper], axis=0)
 
 
-def send_back(rows):
+def send_back_parts(rows):
+    half = lax.axis_index("mp") // (lax.axis_size("mp") // 2)
+    frames = rows.shape[0] // 2
+    lower, upper = rows[:frames], rows[frames:]
+    return jnp.where(half == 0, lower, upper), jnp.where(half == 0, upper, lower)
+
+
+def send_straight(rows):
     count = lax.axis_size("mp")
     group = count // 2
-    half = lax.axis_index("mp") // group
-    frames = rows.shape[0] // 2
-    lower, upper = rows[:frames], rows[frames:]
-    straight = [(i // 2 + (group if i % 2 else 0), i) for i in range(count)]
-    crossed = [(i // 2 + (0 if i % 2 else group), i) for i in range(count)]
-    return (
-        lax.ppermute(jnp.where(half == 0, lower, upper), "mp", straight),
-        lax.ppermute(jnp.where(half == 0, upper, lower), "mp", crossed),
-    )
+    return lax.ppermute(
+        rows, "mp", [(i // 2 + (group if i % 2 else 0), i) for i in range(count)]
+    )
+
+
+def send_crossed(rows):
+    count = lax.axis_size("mp")
+    group = count // 2
+    return lax.ppermute(
+        rows, "mp", [(i // 2 + (0 if i % 2 else group), i) for i in range(count)]
+    )
+
+
+def send_back(rows):
+    first, second = send_back_parts(rows)
+    return send_straight(first), send_crossed(second)
 
 
 def join_back(got_a, got_b):
@@ -153,7 +167,7 @@
     return small
 
 
-def spread_rounds(piece, middle, late, halves, far_weight, extras):
+def spread_rounds(piece, small, middle, late, halves, far_weight, counts):
     far_bit = lax.axis_size("mp") // 2
     if not rounds_fit():
         parts = spread_z(piece)
@@ -166,71 +180,71 @@
         blocks = (near, swap(near, "mp", 1), far, swap(far, "mp", 1))
         return (
             blocks,
+            spread_small(small[None]),
             joined_z(spread_z(middle)),
             joined_z(spread_z(late)),
             send_halves(*halves),
             swap(far_weight, "mp", far_bit),
-            (spread_small(extras[0]), *extras[1:]),
-        )
-    small, rest = extras[0], list(extras[1:])
-    near, far, middle, got, *rest = hold(
+            counts,
+        )
+    small = jnp.stack([small, swap(small, "mp", 1)])
+    near, far, halves, got, counts, middle, late = hold(
         (
             swap(piece, "mp", 2),
             swap(piece, "mp", 4),
+            halves,
+            swap(small, "mp", 2),
+            counts,
             middle,
-            swap(small, "mp", 1),
-            *rest,
+            late,
         )
     )
     small = jnp.concatenate([small, got], axis=0)
     part_a = jnp.concatenate([piece, near], axis=1)
-    a_x, a_y, far_near, mid_near, mid_far, late, far_weight, got = hold(
+    a_x, a_y, far_near, far_weight, small, halves = hold(
         (
             swap(part_a, "dp", 1),
             swap(part_a, "dp", 2),
             swap(far, "mp", 2),
-            swap(middle, "mp", 2),
-            swap(middle, "mp", 4),
-            late,
             far_weight,
-            swap(small, "mp", 2),
-        )
-    )
-    small = jnp.concatenate([small, got], axis=0)
+            small,
+            send_halves(*halves),
+        )
+    )
     part_b = jnp.concatenate([far, far_near], axis=1)
-    b_x, b_y, a_0, a_1, mid_both, late_near, late, far_weight, got, *halves = hold(
+    ahead = jnp.concatenate([middle.reshape(2, -1, middle.shape[-1]), late], axis=1)
+    b_x, b_y, a_0, a_1, far_weight, ahead = hold(
         (
             swap(part_b, "dp", 1),
             swap(part_b, "dp", 2),
             swap(a_y[0], "dp", 1),
             swap(a_x[1], "dp", 2),
-            swap(mid_far, "mp", 2),
-            swap(late, "mp", 2),
-            late,
             swap(far_weight, "mp", 4),
-            swap(small, "mp", 4),
-            *halves,
-        )
-    )
-    small = jnp.concatenate([small, got], axis=0)
+            ahead,
+        )
+    )
     all_a = jnp.concatenate([part_a, a_x, a_y, jnp.stack([a_0, a_1])], axis=1)
-    b_0, b_1, other_a, late, *halves = hold(
+    b_0, b_1, other_a, ahead_near, mid_far, got = hold(
         (
             swap(b_y[0], "dp", 1),
             swap(b_x[1], "dp", 2),
             swap(all_a, "mp", 1),
-            late,
-            *send_halves(*halves),
-        )
-    )
+            swap(ahead, "mp", 2),
+            swap(middle, "mp", 4),
+            swap(small, "mp", 4),
+        )
+    )
+    small = jnp.concatenate([small, got], axis=0)
+    cut = ahead.shape[1] - late.shape[1]
     all_b = jnp.concatenate([part_b, b_x, b_y, jnp.stack([b_0, b_1])], axis=1)
     return (
         (all_a, other_a, all_b, swap(all_b, "mp", 1)),
-        joined_z({0: middle, 2: mid_near, 4: mid_far, 6: mid_both}),
-        (late, late_near),
+        small,
+        {0: middle, 2: ahead_near[:, :cut].reshape(middle.shape), 4: mid_far},
+        {0: late, 2: ahead_near[:, cut:]},
         halves,
         far_weight,
-        (small, *rest),
+        counts,
     )
 
 
@@ -297,14 +311,13 @@
 
 
 def combine_everywhere(rows, combine, beside=None):
-    step = 0
-    for axis in ("dp", "mp"):
-        for bit in bits_of(lax.axis_size(axis)):
-            got = swap(rows, axis, bit)
-            if beside is not None and step < len(beside):
-                got, beside[step] = hold((got, beside[step]))
-                step += 1
-            rows = combine(rows, got)
+    order = [("mp", bit) for bit in bits_of(lax.axis_size("mp"))]
+    order[1:1] = [("dp", bit) for bit in bits_of(lax.axis_size("dp"))]
+    for step, (axis, bit) in enumerate(order):
+        got = swap(rows, axis, bit)
+        if beside is not None and step < len(beside) and beside[step] is not None:
+            got, beside[step] = hold((got, beside[step]))
+        rows = combine(rows, got)
     return rows
 
 
@@ -365,7 +378,7 @@
     return (lane // HEAD) == head
 
 
-def attend_kernel(q_ref, k_ref, v_ref, bias_ref, out_ref, lse_ref):
+def attend_kernel(q_ref, k_ref, v_ref, bias_ref, out_ref, wide_ref, lse_ref):
     query, key, value = q_ref[...], k_ref[...], v_ref[...]
     bias = bias_ref[...]
     factor = LOG2E / math.sqrt(HEAD)
@@ -376,11 +389,12 @@
         row_max = jnp.max(scores, axis=-1, keepdims=True)
         shifted = jnp.exp2(scores - row_max)
         total = jnp.sum(shifted, axis=-1, keepdims=True)
-        probs = (shifted * (1.0 / total)).astype(BF)
-        mixed.append(dot_nn(probs, value))
+        mixed.append(dot_nn(shifted.astype(BF), value) * (1.0 / total))
         logs.append(row_max + jnp.log2(total))
     first = pair_mask(mixed[0].shape, 0)
-    out_ref[...] = jnp.where(first, mixed[0], mixed[1]).astype(BF)
+    wide = jnp.where(first, mixed[0], mixed[1])
+    wide_ref[...] = wide
+    out_ref[...] = wide.astype(BF)
     lse_ref[...] = jnp.where(first, logs[0], logs[1])
 
 
@@ -393,12 +407,13 @@
         attend_kernel,
         grid=(pairs, frames // block),
         in_specs=[rows_spec, whole_spec, whole_spec, pl.BlockSpec((1, frames), lambda p, i: (0, 0))],
-        out_specs=[rows_spec, rows_spec],
+        out_specs=[rows_spec, rows_spec, rows_spec],
         out_shape=[
             jax.ShapeDtypeStruct((frames, columns), BF),
             jax.ShapeDtypeStruct((frames, columns), F32),
+            jax.ShapeDtypeStruct((frames, columns), F32),
         ],
-        compiler_params=pltpu.CompilerParams(vmem_limit_bytes=48 * 1024 * 1024),
+        compiler_params=pltpu.CompilerParams(vmem_limit_bytes=56 * 1024 * 1024),
         cost_estimate=pl.CostEstimate(
             flops=8 * frames * frames * columns,
             bytes_accessed=12 * frames * columns,
@@ -409,7 +424,7 @@
 
 
 def attend_back_kernel(
-    q_ref, k_ref, v_ref, g_ref, lse_ref, bias_ref, dq_ref, dk_ref, dv_ref, dk_acc, dv_acc
+    q_ref, k_ref, v_ref, g_ref, wide_ref, lse_ref, bias_ref, dq_ref, dk_ref, dv_ref, dk_acc, dv_acc
 ):
     step = pl.program_id(1)
     query, key, value, grad = q_ref[...], k_ref[...], v_ref[...], g_ref[...]
@@ -417,7 +432,8 @@
     lse = lse_ref[...]
     factor = LOG2E / math.sqrt(HEAD)
     scale = 1.0 / math.sqrt(HEAD)
-    dq, dk, dv = [], [], []
+    both = grad.astype(F32) * wide_ref[...]
+    dq, new_dk, new_dv = [], 0.0, 0.0
     for head in range(2):
         mask = pair_mask(query.shape, head)
         query_h = jnp.where(mask, query, jnp.zeros_like(query))
@@ -425,15 +441,13 @@
         scores = dot_nt(query_h, key) * factor + bias
         probs = jnp.exp2(scores - lse[:, head * HEAD : head * HEAD + 1])
         grad_probs = dot_nt(grad_h, value)
-        row_dot = jnp.sum(probs * grad_probs, axis=-1, keepdims=True)
+        row_dot = jnp.sum(jnp.where(mask, both, 0.0), axis=-1, keepdims=True)
         grad_scores = (probs * (grad_probs - row_dot)).astype(BF)
-        dv.append(dot_tn(probs.astype(BF), grad_h))
+        new_dv = new_dv + dot_tn(grad_h, probs.astype(BF))
         dq.append(dot_nn(grad_scores, key))
-        dk.append(dot_tn(grad_scores, query_h))
+        new_dk = new_dk + dot_tn(query_h, grad_scores)
     first = pair_mask(dq[0].shape, 0)
     dq_ref[...] = (jnp.where(first, dq[0], dq[1]) * scale).astype(BF)
-    new_dk = dk[0] + dk[1]
-    new_dv = dv[0] + dv[1]
 
     @pl.when(step == 0)
     def _():
@@ -447,11 +461,11 @@
 
     @pl.when(step == pl.num_programs(1) - 1)
     def _():
-        dk_ref[...] = (dk_acc[...] * scale).astype(BF)
-        dv_ref[...] = dv_acc[...].astype(BF)
-
-
-def attend_backward(query, key, value, grad, lse, bias, block):
+        dk_ref[...] = (dk_acc[...] * scale).T.astype(BF)
+        dv_ref[...] = dv_acc[...].T.astype(BF)
+
+
+def attend_backward(query, key, value, grad, wide, lse, bias, block):
     frames, columns = query.shape
     pairs = columns // (2 * HEAD)
     rows_spec = pl.BlockSpec((block, 2 * HEAD), lambda p, i: (i, p))
@@ -466,22 +480,23 @@
             whole_spec,
             rows_spec,
             rows_spec,
+            rows_spec,
             pl.BlockSpec((1, frames), lambda p, i: (0, 0)),
         ],
         out_specs=[rows_spec, whole_spec, whole_spec],
         out_shape=[shape, shape, shape],
         scratch_shapes=[
-            pltpu.VMEM((frames, 2 * HEAD), F32),
-            pltpu.VMEM((frames, 2 * HEAD), F32),
+            pltpu.VMEM((2 * HEAD, frames), F32),
+            pltpu.VMEM((2 * HEAD, frames), F32),
         ],
-        compiler_params=pltpu.CompilerParams(vmem_limit_bytes=48 * 1024 * 1024),
+        compiler_params=pltpu.CompilerParams(vmem_limit_bytes=56 * 1024 * 1024),
         cost_estimate=pl.CostEstimate(
             flops=20 * frames * frames * columns,
             bytes_accessed=20 * frames * columns,
             transcendentals=frames * frames * columns // HEAD,
         ),
         name="attend_backward",
-    )(query, key, value, grad, lse, bias)
+    )(query, key, value, grad, wide, lse, bias)
 
 
 def add_parts_kernel(one_ref, got_one_ref, two_ref, got_two_ref, out_ref):
@@ -630,27 +645,31 @@
     first = halo - taps // 2
     lay_out(gpadded, gbefore_ref, grad_ref, gafter_ref, halo)
     lay_out(padded, before_ref, rows_ref, after_ref, halo)
-    grad = grad_ref[...]
-    total = jnp.zeros((count, lanes), F32)
-    for phase in range(8):
-        more = (taps - 1 - phase) // 8
-        stop = first + phase + count + 8 * more
-        gbase = gpadded[first + phase : stop]
-        base = padded[first + phase : stop]
-        for step in range(more + 1):
-            tap = 8 * step + phase
-            back = taps - 1 - tap
-            total = total + gbase[8 * step : 8 * step + count] * taps_ref[back : back + 1]
-            product = grad * base[8 * step : 8 * step + count]
-            gtaps_ref[tap : tap + 1] = jnp.sum(product, axis=0, keepdims=True)
-    grad_gated = total * visible_ref[...]
-    logistic = logistic_ref[...]
-    gvalue = (grad_gated * logistic).astype(BF)
-    ggate = (grad_gated * value_ref[...] * logistic * (1.0 - logistic)).astype(BF)
-    gvalue_ref[...] = gvalue
-    ggate_ref[...] = ggate
-    gbias_ref[0:1] = jnp.sum(gvalue.astype(F32), axis=0, keepdims=True)
-    gbias_ref[1:2] = jnp.sum(ggate.astype(F32), axis=0, keepdims=True)
+    tap_rows = taps_ref[...]
+    sums = [jnp.zeros((8, lanes), F32) for _ in range(taps)]
+    tile = math.gcd(count, 32)
+    gvalue, ggate = 0.0, 0.0
+    for start in range(0, count, tile):
+        here = slice(start, start + tile)
+        grad = grad_ref[here]
+        total = jnp.zeros((tile, lanes), F32)
+        for tap in range(taps):
+            there = slice(first + start + tap, first + start + tap + tile)
+            total = total + gpadded[there] * tap_rows[taps - 1 - tap : taps - tap]
+            product = (grad * padded[there]).reshape(tile // 8, 8, lanes)
+            sums[tap] = sums[tap] + jnp.sum(product, axis=0)
+        grad_gated = total * visible_ref[here]
+        logistic = logistic_ref[here]
+        value_part = (grad_gated * logistic).astype(BF)
+        gate_part = (grad_gated * value_ref[here] * logistic * (1.0 - logistic)).astype(BF)
+        gvalue_ref[here] = value_part
+        ggate_ref[here] = gate_part
+        gvalue = gvalue + jnp.sum(value_part.astype(F32), axis=0, keepdims=True)
+        ggate = ggate + jnp.sum(gate_part.astype(F32), axis=0, keepdims=True)
+    for tap in range(taps):
+        gtaps_ref[tap : tap + 1] = jnp.sum(sums[tap], axis=0, keepdims=True)
+    gbias_ref[0:1] = gvalue
+    gbias_ref[1:2] = ggate
     gbias_ref[2:] = jnp.zeros((6, lanes), F32)
 
 
@@ -779,7 +798,7 @@
     q = m % group
     width = frames.shape[2]
     columns = width // mp
-    rows_local = 2 * frames.shape[1]
+    rows_local = 2 * mask_flags.shape[1]
     hidden_q = ffa_b_in.shape[0] // dp
     chan_q = columns // dp
     taps = conv_w_depth.shape[0]
@@ -793,10 +812,10 @@
             conv_w_depth,
             batch_scale[None],
             batch_shift[None],
+            att_b_qv,
         ],
         axis=0,
     )
-    per = ffa_b_in.shape[0] // columns
     low = mp // 4
 
     def relative_bias(far, near_core):
@@ -836,26 +855,30 @@
     valid_count = jnp.sum(lengths).astype(F32)
     for bit in bits_of(dp):
         valid_count = valid_count + swap(valid_count, "dp", bit)
-    gathered, mid_z, late_z, halves, w_other, extras = spread_rounds(
+    flags = jnp.pad(mask_flags.astype(BF), ((0, 0), (0, 16 * width - mask_flags.shape[1])))
+    frames = jnp.concatenate([frames, flags.reshape(2, 16, width)], axis=1)
+    per = ffa_b_in.shape[0] // columns
+    gathered, small, mid_z, late_z, halves, w_other, valid_count = spread_rounds(
         jnp.stack(hidden_pieces(ffa_w_in, ffa_w_out)),
+        jnp.pad(small, ((0, -small.shape[0] % 16), (0, 0))).reshape(-1, width),
         jnp.stack([channel_piece(rows) for rows in kinds]),
         jnp.stack(hidden_pieces(ffb_w_in, ffb_w_out)),
         split_halves(frames),
         att_w_qkv,
-        (
-            small[None],
-            swap(att_b_qv, "mp", group),
-            join_halves(*send_halves(*split_halves(mask_flags))),
-            valid_count,
-        ),
-    )
-    small, b_other, flag_rows, valid_count = extras
+        valid_count,
+    )
+    small = small.reshape(mp, -1, columns)[:, : 2 * per + 6 + taps]
     bias_rel = small[:, :per].reshape(mp, dp, hidden_q)[:, jnp.arange(dp) ^ d]
     small = small[jnp.arange(mp) ^ m]
     bias_b = hidden_bias(small[:, per : 2 * per])
-    conv_small = to_canon(jnp.moveaxis(small[:, 2 * per :], 0, 1).reshape(-1, width))
-    rows_in = join_halves(*halves)
-    flag_rows = flag_rows.astype(F32)[:, None]
+    small = small[:, 2 * per :]
+    conv_small = to_canon(jnp.moveaxis(small[:, : 4 + taps], 0, 1).reshape(-1, width))
+    b_qv = jnp.moveaxis(small[:, 4 + taps :], 0, 1).reshape(2, 2, group, columns)
+    b_qv = lax.dynamic_index_in_dim(b_qv, q, 2, keepdims=False).reshape(2, -1)
+    frames_local = mask_flags.shape[1]
+    rows_in = join_halves(*(part[:frames_local] for part in halves))
+    flag_rows = [part[frames_local:].reshape(-1)[:frames_local, None] for part in halves]
+    flag_rows = join_halves(*flag_rows).astype(F32)
     c_b_in = [conv_small[0:1], conv_small[1:2]]
     c_depth = jnp.pad(conv_small[2 : 2 + taps], ((0, -taps % 8), (0, 0)))
     c_scale = conv_small[2 + taps : 3 + taps]
@@ -863,15 +886,9 @@
     blocks_a = [
         (gathered[k][0], gathered[k][1], relative_bias(k // 2, k % 2)) for k in range(4)
     ]
-    mid_own = lax.all_gather(mid_z, "dp", axis=1, tiled=True)
-
-    w_qkv = jnp.concatenate(
-        [jnp.where(half == 0, att_w_qkv, w_other), jnp.where(half == 0, w_other, att_w_qkv)], axis=2
-    )
-    b_qv = jnp.concatenate(
-        [jnp.where(half == 0, att_b_qv, b_other), jnp.where(half == 0, b_other, att_b_qv)], axis=1
-    )
-
+    if not rounds_fit():
+        mid_own = lax.all_gather(mid_z, "dp", axis=1, tiled=True)
+        late_own = lax.all_gather(late_z, "dp", axis=1, tiled=True)
 
     length = lax.dynamic_index_in_dim(lengths, half, 0, keepdims=False)
     place = q * rows_local + jnp.arange(rows_local)
@@ -880,26 +897,40 @@
     key_bias = jnp.where(key_place < length, 0.0, -1e30).astype(F32)
 
     resid_a = rows_in.astype(F32) + flag_rows * mask_embed
-    beside = [swap(late_z[0], "mp", 4)] if rounds_fit() else None
-    branch, saved_a = ffn_forward(resid_a, ffa_gain, ffa_shift, blocks_a, ffa_b_out, beside)
+    if rounds_fit():
+        beside = [swap(mid_z[4], "mp", 2)]
+        branch, saved_a = ffn_forward(resid_a, ffa_gain, ffa_shift, blocks_a, ffa_b_out, beside)
+        mid_z = joined_z({**mid_z, 6: beside[0]})
+        mid_own = lax.all_gather(mid_z, "dp", axis=1, tiled=True)
+    else:
+        branch, saved_a = ffn_forward(resid_a, ffa_gain, ffa_shift, blocks_a, ffa_b_out)
     resid_b = resid_a + 0.5 * branch
 
     normed, att_unit, att_inv = norm_forward(resid_b, att_gain, att_shift)
-    blocks = spread_blocks(normed.astype(BF), group)
-    *blocks, mid_own, beside = hold((*blocks, mid_own, beside))
+    att_act = normed.astype(BF)
     if rounds_fit():
-        far_near = swap(beside[0], "mp", 2)
-    mid_other = swap(mid_own, "mp", 1)
+        near, by_core_act, late_far = hold(
+            (swap(att_act, "mp", 2), swap(att_act, "mp", 1), swap(late_z[0], "mp", 4))
+        )
+        blocks = [att_act, by_core_act, near, swap(near, "mp", 1)]
+    else:
+        blocks = spread_blocks(att_act, group)
+    w_qkv = jnp.concatenate(
+        [jnp.where(half == 0, att_w_qkv, w_other), jnp.where(half == 0, w_other, att_w_qkv)], axis=2
+    )
     att_rows = jnp.concatenate(blocks, axis=0)
     query = (dot_nn(att_rows, w_qkv[0]) + b_qv[0]).astype(BF)
     key = dot_nn(att_rows, w_qkv[1]).astype(BF)
     value = (dot_nn(att_rows, w_qkv[2]) + b_qv[1]).astype(BF)
     if rounds_fit():
-        query, key, value, far_near = hold((query, key, value, far_near))
-        late_z = joined_z({0: late_z[0], 2: late_z[1], 4: beside[0], 6: far_near})
-    late_own = lax.all_gather(late_z, "dp", axis=1, tiled=True)
-    block = rows_local
-    mixed_cols, lse = attend_forward(query, key, value, key_bias, block)
+        query, key, value, late_both, mid_own = hold(
+            (query, key, value, swap(late_far, "mp", 2), mid_own)
+        )
+        late_z = joined_z({**late_z, 4: late_far, 6: late_both})
+        late_own = lax.all_gather(late_z, "dp", axis=1, tiled=True)
+    block = group * rows_local // 2
+    mixed_cols, mixed_wide, lse = attend_forward(query, key, value, key_bias, block)
+    mid_other = swap(mid_own, "mp", 1)
     parts = [mixed_cols[r * rows_local : (r + 1) * rows_local] for r in range(group)]
     parts = exchange_blocks(parts)
     mid = jnp.stack(
@@ -936,11 +967,8 @@
 
     gated_halos = halos(gated)
     depth, stats = depth_forward(gated, gated_halos, c_depth, visible, taps)
-    depth, stats, late_own, *cot_halves = hold((depth, stats, late_own, *cot_halves))
+    depth, stats, *cot_halves = hold((depth, stats, *cot_halves))
     cot_rows = join_halves(*cot_halves)
-    late_own = late_own.reshape(2, -1, width)
-    late_other = swap(late_own, "mp", 1)
-    blocks_b = [(late_own[0], late_own[1], bias_b[0]), (late_other[0], late_other[1], bias_b[1])]
 
     def join(one, two):
         both = jnp.maximum(one[0:1] + two[0:1], 1.0)
@@ -955,7 +983,11 @@
             axis=0,
         )
 
-    stats = combine_everywhere(stats, join)
+    beside = [None, None, None, None, late_own]
+    stats = combine_everywhere(stats, join, beside)
+    late_own = beside[4].reshape(2, -1, width)
+    late_other = swap(late_own, "mp", 1)
+    blocks_b = [(late_own[0], late_own[1], bias_b[0]), (late_other[0], late_other[1], bias_b[1])]
     batch_mean = stats[1:2]
     batch_var = stats[2:3] / valid_count
     inv_batch = lax.rsqrt(batch_var + EPS)
@@ -1039,15 +1071,33 @@
     wide = 2 * columns
     parts = [grad_mixed[:, r * wide : (r + 1) * wide] for r in range(group)]
     grad_cols = jnp.concatenate(exchange_blocks(parts), axis=0)
-    grad_q, grad_k, grad_v = attend_backward(query, key, value, grad_cols, lse, key_bias, block // 2)
-
+    grad_q, grad_k, grad_v = attend_backward(
+        query, key, value, grad_cols, mixed_wide, lse, key_bias, block
+    )
+
+    grad_q, grad_k, grad_v, late_sum = hold((grad_q, grad_k, grad_v, late_sum))
+    late_sum = late_sum.reshape(2, zs, hidden_q, width)
+    late_parts = reordered(jnp.moveaxis(late_sum, 1, 0).reshape(zs, -1, width), m // 2)
+    if rounds_fit():
+        late_got = swap(late_parts[1::2], "mp", 2)
     mid_g = [g_conv_value, g_conv_gate, g_conv_out, g_att_out]
     mid_got = swap(jnp.concatenate([g[1] for g in mid_g], axis=0), "mp", 1)
     grad_all = jnp.concatenate([grad_q, grad_k, grad_v], axis=1)
     w_flat = jnp.concatenate([w_qkv[0], w_qkv[1], w_qkv[2]], axis=1)
     partial = dot_nt(grad_all, w_flat)
     g_qkv = dot_tn(grad_all, att_rows).astype(BF)
-    partial, g_qkv, mid_got, *layer_out = hold((partial, g_qkv, mid_got, *layer_out))
+    partial, *layer_out = hold((partial, *layer_out))
+    partial = [partial[r * rows_local : (r + 1) * rows_local] for r in range(group)]
+    if rounds_fit():
+        got_0, got_1, mid_got = hold(
+            (
+                swap(partial[1].astype(BF), "mp", 1),
+                swap(partial[3].astype(BF), "mp", 1),
+                mid_got,
+            )
+        )
+        to_near = (partial[2] + got_1.astype(F32)).astype(BF)
+        to_near, mid_got, g_qkv = hold((to_near, mid_got, g_qkv))
     mid_got = mid_got.reshape(4, zs, columns, width)
     joint = [
         add_rounded(g[0].reshape(zs, columns, width), got)
@@ -1062,14 +1112,13 @@
             ]
             joint_parts.append(jnp.concatenate(part, axis=0).reshape(joint_rows, width))
         joint_corners = corners(joint_parts)
-    grad_act = collect_blocks(
-        [partial[r * rows_local : (r + 1) * rows_local] for r in range(group)]
-    )
     if rounds_fit():
-        grad_act, late_sum, *joint_corners = hold((grad_act, late_sum, *joint_corners))
+        got, late_got, *joint_corners = hold((swap(to_near, "mp", 2), late_got, *joint_corners))
+        grad_act = partial[0] + got_0.astype(F32) + got.astype(F32)
         joint_sides = sides(joint_parts, *joint_corners)
-    late_sum = late_sum.reshape(2, zs, hidden_q, width)
-    late_parts = reordered(jnp.moveaxis(late_sum, 1, 0).reshape(zs, -1, width), m // 2)
+        late_parts = add_rounded(late_parts[0::2], late_got)
+    else:
+        grad_act = collect_blocks(partial)
     g_qv = jnp.stack(
         [jnp.sum(grad_q, axis=0, dtype=F32), jnp.sum(grad_v, axis=0, dtype=F32)]
     ).reshape(2, 2, 1, columns)
@@ -1096,42 +1145,39 @@
         if k == 3:
             held = hold(held)
             flight["b"] = [swap(held[2], "mp", 1), swap(held[3], "mp", 1)]
-            flight["late"] = swap(late_parts[1::2], "mp", 2)
+            flight["late"] = swap(late_parts[1], "mp", 4)
         elif k == 2:
-            *held, b_in, b_out, side_x, side_y, late_got = hold(
-                (*held, *flight["b"], *joint_sides, flight["late"])
-            )
+            *held, b_in, b_out = hold((*held, *flight["b"]))
             parts = add_parts(held[2], b_in, held[3], b_out, 4)
             flight["b_parts"] = [parts[r].reshape(-1, width) for r in range(4)]
             flight["corners"] = corners(flight["b_parts"])
-            late = add_rounded(late_parts[0::2], late_got)
-            flight["late"] = [late[0], swap(late[1], "mp", 4)]
+        elif k == 1:
+            *held, side_x, side_y, to_x, to_y, late_far = hold(
+                (*held, *joint_sides, *flight["corners"], flight["late"])
+            )
+            flight["late"] = add_rounded(late_parts[0], late_far)
+            b_sides = sides(flight["b_parts"], to_x, to_y)
             flight["mid"], flight["pair"] = joint_pieces(finish(joint_parts, side_x, side_y))
-        elif k == 1:
-            mid = flight["mid"]
-            *held, to_x, to_y, far = hold((*held, *flight["corners"], flight["late"][1]))
-            flight["sides"] = sides(flight["b_parts"], to_x, to_y)
-            flight["late"] = add_rounded(flight["late"][0], far)
-            flight["a"] = [swap(held[2], "mp", 1), swap(held[3], "mp", 1)]
-            flight["mid_got"] = swap(mid[1::2], "mp", 2)
+            mid_got = swap(flight["mid"][1::2], "mp", 2)
+            a_got = [swap(held[2], "mp", 1), swap(held[3], "mp", 1)]
+            flight["k1"] = (*a_got, *b_sides, mid_got)
         else:
-            *held, a_in, a_out, mid_got = hold((*held, *flight["a"], flight["mid_got"]))
+            *held, a_in, a_out, b_x, b_y, mid_got = hold((*held, *flight["k1"]))
             parts = add_parts(held[2], a_in, held[3], a_out, 4)
             flight["a_parts"] = [parts[r].reshape(-1, width) for r in range(4)]
             flight["corners"] = corners(flight["a_parts"])
+            b_sum = finish(flight["b_parts"], b_x, b_y).reshape(2, 2, hidden_q, width)
+            flight["b_sum"] = b_sum[:, 0], swap(b_sum[:, 1], "mp", 2)
             mid = add_rounded(flight["mid"][0::2], mid_got)
-            rows = jnp.concatenate([mid[1], flight["pair"][1]], axis=0)
-            flight["far"] = [
-                jnp.concatenate([mid[0], flight["pair"][0]], axis=0),
-                swap(rows, "mp", 4),
-            ]
+            far = swap(jnp.concatenate([mid[1], flight["pair"][1]], axis=0), "mp", 4)
+            flight["mid"] = jnp.concatenate([mid[0], flight["pair"][0]], axis=0), far
         return held
 
     grad_resid, mats_a, vecs_a = ffn_backward(
         grad_resid, saved_a, ffa_gain, blocks_a, between if rounds_fit() else None
     )
     g_embed = jnp.sum(grad_resid * flag_rows, axis=0, keepdims=True)
-    grad_frames = send_back(grad_resid.astype(BF))
+    back_first, back_second = send_back_parts(grad_resid.astype(BF))
 
     def hidden_order(parts):
         own, other = parts
@@ -1166,59 +1212,57 @@
         )
     )
     if rounds_fit():
-        b_x, b_y, *grad_frames, far, got = hold(
-            (*flight["sides"], *grad_frames, flight["far"][1], swap(small, "dp", 1))
+        b_own, b_near = flight["b_sum"]
+        rest, far = flight["mid"]
+        to_x, to_y, b_near, far, got = hold(
+            (*flight["corners"], b_near, far, swap(small, "dp", 1))
         )
         small = small + got
-        b_sum = finish(flight["b_parts"], b_x, b_y).reshape(2, 2, hidden_q, width)
-        rest = jnp.concatenate([flight["late"], add_rounded(flight["far"][0], far)], axis=0)
-        to_x, to_y, b_near, got, rest = hold(
+        side_x, side_y = sides(flight["a_parts"], to_x, to_y)
+        rest = jnp.concatenate([flight["late"], add_rounded(rest, far)], axis=0)
+        side_x, side_y, b_far, got, rest, back_first, back_second = hold(
             (
-                *flight["corners"],
-                swap(b_sum[:, 1], "mp", 2),
+                side_x,
+                side_y,
+                swap(add_rounded(b_own, b_near), "mp", 4),
                 swap(small, "dp", 2),
                 rest,
+                back_first,
+                back_second,
             )
         )
         small = small + got
-        side_x, side_y = sides(flight["a_parts"], to_x, to_y)
-        b_far, side_x, side_y, got, rest_x, rest_y = hold(
-            (
-                swap(add_rounded(b_sum[:, 0], b_near), "mp", 4),
-                side_x,
-                side_y,
-                swap(small, "mp", 1),
-                rest,
-                rest,
-            )
-        )
-        small = small + got
+        small = small + swap(small, "mp", 1)
         a_sum = finish(flight["a_parts"], side_x, side_y).reshape(2, 2, hidden_q, width)
-        a_near, got, rest_x, rest_y = hold(
+        a_near, rest_x, rest_y, got = hold(
             (
                 swap(a_sum[:, 1], "mp", 2),
+                swap(rest, "dp", 1),
+                swap(rest, "dp", 2),
                 swap(small, "mp", 2),
-                swap(rest_x, "dp", 1),
-                swap(rest_y, "dp", 2),
             )
         )
         small = small + got
+        small, back_first = hold((small + swap(small, "mp", 4), back_first))
         own = a_sum[:, 0].astype(F32) + a_near.astype(F32) + b_far.astype(F32)
         own = own.astype(BF).reshape(-1, width)
         cut = rest.shape[0] // 2
-        by_x, by_y, got, rest_0, rest_1 = hold(
+        by_x, by_y, rest_0, rest_1, back_first, back_second = hold(
             (
                 swap(own, "dp", 1),
                 swap(own, "dp", 2),
-                swap(small, "mp", 4),
                 swap(rest_y[:cut], "dp", 1),
                 swap(rest_x[cut:], "dp", 2),
+                send_straight(back_first),
+                back_second,
             )
         )
-        small = small + got
+        back_second = send_crossed(back_second)
         corner = [swap(by_y[:hidden_q], "dp", 1), swap(by_x[hidden_q:], "dp", 2)]
         first = jnp.stack([own, by_x, by_y, jnp.concatenate(corner, axis=0)])
         rest = jnp.stack([rest, rest_x, rest_y, jnp.concatenate([rest_0, rest_1], axis=0)])
+        late_all = rest[:, : 2 * hidden_q]
+        rest = rest[:, 2 * hidden_q :]
     else:
         joint = jnp.concatenate(joint, axis=0)
         joint = lax.psum_scatter(joint, "dp", scatter_dimension=1, tiled=True)
@@ -1226,19 +1270,20 @@
         total = collect_plain(
             mats_a[0], mats_a[2], jnp.concatenate([late_parts, mid_parts], axis=1), pair
         )
-        first, rest = total[:, : 2 * hidden_q], total[:, 2 * hidden_q :]
+        back_first, back_second = send_straight(back_first), send_crossed(back_second)
+        first, late_all, rest = jnp.split(total, [2 * hidden_q, 4 * hidden_q], axis=1)
         small = combine_everywhere(small, jnp.add)
     if hidden_q % 128 == 0:
         g_ffa_in, g_ffa_out = unpack(first, d, hidden_q, 0)
-        g_ffb_in, g_ffb_out = unpack(rest[:, : 2 * hidden_q], d, hidden_q, 0)
+        g_ffb_in, g_ffb_out = unpack(late_all, d, hidden_q, 0)
     else:
         pairs = []
-        for part in (first, rest[:, : 2 * hidden_q]):
+        for part in (first, late_all):
             part = reordered(part, d).reshape(dp, 2, hidden_q, width).astype(F32)
             part = jnp.moveaxis(part, 1, 0).reshape(2, -1, width)
             pairs += [part[0].T, part[1]]
         g_ffa_in, g_ffa_out, g_ffb_in, g_ffb_out = pairs
-    rest = reordered(rest[:, 2 * hidden_q :], d).reshape(dp, 7, chan_q, width)
+    rest = reordered(rest, d).reshape(dp, 7, chan_q, width)
     rest = jnp.moveaxis(rest, 1, 0).reshape(7, columns, width).astype(F32)
     mid_total = rest[:4]
     g_att_qkv = rest[4:].transpose(0, 2, 1)
@@ -1272,7 +1317,7 @@
     g_conv_w_in = jnp.stack([mid_total[0].T, mid_total[1].T])
     return (
         join_back(*layer_out),
-        join_back(*grad_frames),
+        join_back(back_first, back_second),
         f[3],
         f[0],
         f[1],

time: 851 us -> 794 us (0.933)
  waiting for transfers between devices: 282 us -> 238 us
  starting transfers between devices: 133 us -> 110 us
  matrix products: 126 us -> 148 us
  Pallas kernels: 113 us -> 91.3 us
    ppermute x89 -> x87, waiting for transfers between devices: 251 us -> 224 us  [swap(): return lax.ppermute(values, axis, [(i, i ^ bit) for i in range(count)])]
    ppermute x89 -> x87, starting transfers between devices: 106 us -> 86.1 us  [swap(): return lax.ppermute(values, axis, [(i, i ^ bit) for i in range(count)])]
    all_gather x1, waiting for transfers between devices: 17.5 us -> 0.01 us  [shards(): late_own = lax.all_gather(late_z, 'dp', axis=1, tiled=True)]
    pallas_call x1, Pallas kernels: 49.2 us -> 32.4 us  [attend_backward(): pl.pallas_call(attend_back_kernel, grid=(pairs, frames // block), in_spec...]
    dot_general x19, matrix products: 41.1 us -> 56.9 us  [dot_nn(): lax.dot_general(left, right, (((1,), (0,)), ((), ())), preferred_element_...]
    ppermute x3 -> x2, waiting for transfers between devices: 3.9 us -> 13.5 us  [send_halves(): lax.ppermute(second, 'mp', crossed)]
    unnamed x419 -> x420, local copies, waits for them, and re-layouts: 43.7 us -> 41.6 us
  transfers between devices with their start and end apart: 106 -> 102, of which waited for: 49 -> 47; matrix products, arithmetic and copies ran while one was open for 23% -> 30% of each run, Pallas kernels for 12% -> 11%
where the time goes in v2:
time: 794 us; the launch traced here: 783 us
  waiting for transfers between devices  238 us (30%)
  matrix products  148 us (19%)
  starting transfers between devices  110 us (14%)
  other arithmetic  91.8 us (12%)
  Pallas kernels  91.3 us (11%)
  local copies, waits for them, and re-layouts  84.8 us (11%)
  between operations  19.8 us (2%)
    ppermute x87, waiting for transfers between devices, swap(): return lax.ppermute(values, axis, [(i, i ^ bit) for i in range(count)])  224 us
    ppermute x87, starting transfers between devices, swap(): return lax.ppermute(values, axis, [(i, i ^ bit) for i in range(count)])  86.1 us
    dot_general x19, matrix products, dot_nn(): lax.dot_general(left, right, (((1,), (0,)), ((), ())), preferred_element_...  56.9 us
    dot_general x17, matrix products, dot_nt(): lax.dot_general(left, right, (((1,), (1,)), ((), ())), preferred_element_...  47.2 us
    dot_general x21, matrix products, dot_tn(): lax.dot_general(left, right, (((0,), (0,)), ((), ())), preferred_element_...  43.7 us
    unnamed x420, local copies, waits for them, and re-layouts  41.6 us
    pallas_call x1, Pallas kernels, attend_backward(): pl.pallas_call(attend_back_kernel, grid=(pairs, frames // block), in_spec...  32.4 us
    pallas_call x1, Pallas kernels, attend_forward(): pl.pallas_call(attend_kernel, grid=(pairs, frames // block), in_specs=[ro...  24.8 us
  transfers between devices with their start and end apart: 102, of which 47 were waited for; matrix products, arithmetic and copies ran while one was open for 30% of the time, Pallas kernels for 11%

profile of v2, /device:TPU:0, one launch (start us, length us, event | category | flops | bytes accessed | tf_op | source)
XLA Modules:
  0.0 783.1 jit_solution(8990896273648328995)
XLA Ops:
  33.7 5.1 collective-permute-done.3
  50.4 13.5 %collective-permute-done.10 = bf16[224,1024]{1,0:T(8,128)(2,1)S(1)} collective-permute-done((bf16[224,1024]{1,0:T(8,128)(2,1)}, bf16[224,1024]{1,0:T(8,128)(2,1)S(1)}, u32[]{:S(2)}, u32[]{:S(2)}) %collective-permute-start.10) | collective-permute-done | bytes 458784 | tf_op jit(solution)/shard_map/ppermute | solution.py:78
  67.4 4.7 collective-permute-start.15
  79.1 23.3 %collective-permute-done.13 = bf16[256,1024]{1,0:T(8,128)(2,1)S(1)} collective-permute-done((bf16[256,1024]{1,0:T(8,128)(2,1)S(1)}, bf16[256,1024]{1,0:T(8,128)(2,1)S(1)}, u32[]{:S(2)}, u32[]{:S(2)}) %collective-permute-start.13) | collective-permute-done | bytes 524320 | tf_op jit(solution)/shard_map/ppermute | solution.py:32
  116.1 6.2 collective-permute-done.20
  123.4 11.5 %collective-permute-done.21 = f32[4,6,1024]{2,1,0:T(8,128)S(1)} collective-permute-done((f32[4,6,1024]{2,1,0:T(8,128)S(1)}, f32[4,6,1024]{2,1,0:T(8,128)S(1)}, u32[]{:S(2)}, u32[]{:S(2)}) %collective-permute-start.21) | collective-permute-done | bytes 98336 | tf_op jit(solution)/shard_map/ppermute | solution.py:32
  134.9 6.2 collective-permute-done.19
  175.9 29.8 %collective-permute-done.26 = bf16[2,128,1024]{2,1,0:T(8,128)(2,1)S(1)} collective-permute-done((bf16[2,128,1024]{2,1,0:T(8,128)(2,1)S(1)}, bf16[2,128,1024]{2,1,0:T(8,128)(2,1)S(1)}, u32[]{:S(2)}, u32[]{:S(2)}) %collective-permute-start.26) | collective-permute-done | bytes 524320 | tf_op jit(solution)/shard_map/ppermute | solution.py:32
  233.7 24.8 %attend_forward.1 = (bf16[1664,256]{1,0:T(8,128)(2,1)}, f32[1664,256]{1,0:T(8,128)}, f32[1664,256]{1,0:T(8,128)}) custom-call(bf16[1664,256]{1,0:T(8,128)(2,1)} %fusion.6.q_ref, bf16[1664,256]{1,0:T(8,128)(2,1)} %convolution_convert_fusion.4.k_ref, bf16[1664,256]{1,0:T(8,128)(2,1)} %fusion.7.v_ref, f32[1,1664]{1,0:T(1,128)} %select_n.385.bias_ref), custom_call_target="tpu_custom_call" | custom-call | flops 5670699008 | bytes 5111808 | tf_op jit(solution)/shard_map/attend_forward/pallas_call | solution.py:406
  272.2 5.0 collective-permute-start.35
  290.5 7.7 depth_forward.1
  354.5 4.8 convert_reduce_fusion
  359.3 5.3 multiply_reduce_fusion.5
  384.4 5.2 collective-permute-done.46.got_two_ref
  389.7 5.6 add_parts.3
  417.8 11.7 %depth_backward.1 = (bf16[416,1024]{1,0:T(8,128)(2,1)}, bf16[416,1024]{1,0:T(8,128)(2,1)}, f32[32,1024]{1,0:T(8,128)}, f32[8,1024]{1,0:T(8,128)}) custom-call(f32[16,1024]{1,0:T(8,128)} %copy-done.112, f32[416,1024]{1,0:T(8,128)} %copy-done.20, f32[16,1024]{1,0:T(8,128)} %collective-permute-done.51.gafter_ref, f32[16,1024]{1,0:T(8,128)} %copy-done.101, ...), custom_call_target="tpu_custom_call" | custom-call | flops 52822016 | bytes 10223616 | tf_op jit(solution)/shard_map/depth_backward/pallas_call | solution.py:684
  451.9 32.4 %attend_backward.1 = (bf16[1664,256]{1,0:T(8,128)(2,1)}, bf16[1664,256]{1,0:T(8,128)(2,1)}, bf16[1664,256]{1,0:T(8,128)(2,1)}) custom-call(bf16[1664,256]{1,0:T(8,128)(2,1)} %fusion.6.q_ref, bf16[1664,256]{1,0:T(8,128)(2,1)} %convolution_convert_fusion.4.k_ref, bf16[1664,256]{1,0:T(8,128)(2,1)} %fusion.7.v_ref, bf16[1664,256]{1,0:T(8,128)(2,1)} %pad_maximum_fusion.25.g_ref, ...), custom_call_target="tpu_custom_call" | custom-call | flops 14176747520 | bytes 8519680 | tf_op jit(solution)/shard_map/attend_backward/pallas_call | solution.py:474
  527.2 9.6 %collective-permute-done.62 = bf16[352,1024]{1,0:T(8,128)(2,1)} collective-permute-done((bf16[352,1024]{1,0:T(8,128)(2,1)}, bf16[352,1024]{1,0:T(8,128)(2,1)}, u32[]{:S(2)}, u32[]{:S(2)}) %collective-permute-start.62) | collective-permute-done | bytes 720928 | tf_op jit(solution)/shard_map/ppermute | solution.py:32
  592.4 7.5 collective-permute-done.68
  658.6 11.7 %collective-permute-done.79 = bf16[224,1024]{1,0:T(8,128)(2,1)} collective-permute-done((bf16[224,1024]{1,0:T(8,128)(2,1)}, bf16[224,1024]{1,0:T(8,128)(2,1)}, u32[]{:S(2)}, u32[]{:S(2)}) %collective-permute-start.79) | collective-permute-done | bytes 458784 | tf_op jit(solution)/shard_map/ppermute | solution.py:32
  678.8 21.8 %collective-permute-done.84 = f32[58,1024]{1,0:T(8,128)S(1)} collective-permute-done((f32[58,1024]{1,0:T(8,128)S(1)}, f32[58,1024]{1,0:T(8,128)S(1)}, u32[]{:S(2)}, u32[]{:S(2)}) %collective-permute-start.84) | collective-permute-done | bytes 237600 | tf_op jit(solution)/shard_map/ppermute | solution.py:32
  710.1 14.9 %collective-permute-done.89 = f32[58,1024]{1,0:T(8,128)S(1)} collective-permute-done((f32[58,1024]{1,0:T(8,128)S(1)}, f32[58,1024]{1,0:T(8,128)S(1)}, u32[]{:S(2)}, u32[]{:S(2)}) %collective-permute-start.89) | collective-permute-done | bytes 237600 | tf_op jit(solution)/shard_map/ppermute | solution.py:32
  729.8 9.7 %collective-permute-done.94 = f32[58,1024]{1,0:T(8,128)S(1)} collective-permute-done((f32[58,1024]{1,0:T(8,128)S(1)}, f32[58,1024]{1,0:T(8,128)S(1)}, u32[]{:S(2)}, u32[]{:S(2)}) %collective-permute-start.94) | collective-permute-done | bytes 237600 | tf_op jit(solution)/shard_map/ppermute | solution.py:32
  744.0 5.6 collective-permute-done.92
  (945 shorter events, 479.5 us)
Async XLA Ops:
  7.2 219.6 %all-gather.3.cloned.1.call-start = ((), (), s32[]{:S(2)}) async-start(), calls=%async_computation.1 | async-start | bytes 5242880 | tf_op jit(solution)/shard_map/all_gather | solution.py:904
  65.3 40.1 %collective-permute-start.11 = (bf16[2,256,1024]{2,1,0:T(8,128)(2,1)S(1)}, bf16[2,256,1024]{2,1,0:T(8,128)(2,1)S(1)}, u32[]{:S(2)}, u32[]{:S(2)}) collective-permute-start(bf16[2,256,1024]{2,1,0:T(8,128)(2,1)S(1)} %get-tuple-element.563), channel_id=1, source_target_pairs={{0,8},{8,0},{16,24},{24,16},{1,9},{9,1},{17,25},{25,17},{2,10},{10... | collective-permute-start | bytes 3145736 | tf_op jit(solution)/shard_map/ppermute | solution.py:32
  66.0 39.4 %collective-permute-start.12 = (bf16[2,256,1024]{2,1,0:T(8,128)(2,1)S(1)}, bf16[2,256,1024]{2,1,0:T(8,128)(2,1)S(1)}, u32[]{:S(2)}, u32[]{:S(2)}) collective-permute-start(bf16[2,256,1024]{2,1,0:T(8,128)(2,1)S(1)} %get-tuple-element.563), channel_id=1, source_target_pairs={{0,16},{8,24},{16,0},{24,8},{1,17},{9,25},{17,1},{25,9},{2,18},{10... | collective-permute-start | bytes 3145736 | tf_op jit(solution)/shard_map/ppermute | solution.py:32
  67.4 38.0 %collective-permute-start.15 = (bf16[3,1024,128]{2,1,0:T(8,128)(2,1)S(1)}, bf16[3,1024,128]{2,1,0:T(8,128)(2,1)S(1)}, u32[]{:S(2)}, u32[]{:S(2)}) collective-permute-start(bf16[3,1024,128]{2,1,0:T(8,128)(2,1)S(1)} %copy-done.84), channel_id=1, source_target_pairs={{0,4},{1,5},{2,6},{3,7},{4,0},{5,1},{6,2},{7,3},{8,12},{9,13},{10,... | collective-permute-start | bytes 2359304 | tf_op jit(solution)/shard_map/ppermute | solution.py:32
  72.1 30.4 %collective-permute-start.13 = (bf16[256,1024]{1,0:T(8,128)(2,1)S(1)}, bf16[256,1024]{1,0:T(8,128)(2,1)S(1)}, u32[]{:S(2)}, u32[]{:S(2)}) collective-permute-start(bf16[256,1024]{1,0:T(8,128)(2,1)S(1)} %slice_bitcast_fusion.58), channel_id=1, source_target_pairs={{0,8},{8,0},{16,24},{24,16},{1,9},{9,1},{17,25},{25,17},{2,10},{10... | collective-permute-start | bytes 1572872 | tf_op jit(solution)/shard_map/ppermute | solution.py:32
  73.7 29.1 %collective-permute-start.14 = (bf16[256,1024]{1,0:T(8,128)(2,1)S(1)}, bf16[256,1024]{1,0:T(8,128)(2,1)S(1)}, u32[]{:S(2)}, u32[]{:S(2)}) collective-permute-start(bf16[256,1024]{1,0:T(8,128)(2,1)S(1)} %slice_bitcast_fusion.57), channel_id=1, source_target_pairs={{0,16},{8,24},{16,0},{24,8},{1,17},{9,25},{17,1},{25,9},{2,18},{10... | collective-permute-start | bytes 1572872 | tf_op jit(solution)/shard_map/ppermute | solution.py:32
  107.3 33.8 %collective-permute-start.18 = (bf16[2,1024,1024]{2,1,0:T(8,128)(2,1)}, bf16[2,1024,1024]{2,1,0:T(8,128)(2,1)}, u32[]{:S(2)}, u32[]{:S(2)}) collective-permute-start(bf16[2,1024,1024]{2,1,0:T(8,128)(2,1)} %maximum_dynamic-update-slice_fusion), channel_id=1, source_target_pairs={{0,1},{1,0},{2,3},{3,2},{4,5},{5,4},{6,7},{7,6},{8,9},{9,8},{10,11... | collective-permute-start | bytes 12582920 | tf_op jit(solution)/shard_map/ppermute | solution.py:32
  160.6 162.5 %all-gather.5.cloned.1.call-start = ((), (), s32[]{:S(2)}) async-start(), calls=%async_computation.2 | async-start | bytes 10485760 | tf_op jit(solution)/shard_map/all_gather | solution.py:930
  174.0 32.8 %collective-permute-start.24 = (bf16[416,1024]{1,0:T(8,128)(2,1)S(1)}, bf16[416,1024]{1,0:T(8,128)(2,1)}, u32[]{:S(2)}, u32[]{:S(2)}) collective-permute-start(bf16[416,1024]{1,0:T(8,128)(2,1)S(1)} %add_convert_fusion.9), channel_id=1, source_target_pairs={{0,2},{1,3},{2,0},{3,1},{4,6},{5,7},{6,4},{7,5},{8,10},{9,11},{10,... | collective-permute-start | bytes 2555912 | tf_op jit(solution)/shard_map/ppermute | solution.py:32
  175.9 30.8 %collective-permute-start.25 = (bf16[416,1024]{1,0:T(8,128)(2,1)S(1)}, bf16[416,1024]{1,0:T(8,128)(2,1)S(1)}, u32[]{:S(2)}, u32[]{:S(2)}) collective-permute-start(bf16[416,1024]{1,0:T(8,128)(2,1)S(1)} %add_convert_fusion.9), channel_id=1, source_target_pairs={{0,1},{1,0},{2,3},{3,2},{4,5},{5,4},{6,7},{7,6},{8,9},{9,8},{10,11... | collective-permute-start | bytes 2555912 | tf_op jit(solution)/shard_map/ppermute | solution.py:32
  175.9 29.8 %collective-permute-start.26 = (bf16[2,128,1024]{2,1,0:T(8,128)(2,1)S(1)}, bf16[2,128,1024]{2,1,0:T(8,128)(2,1)S(1)}, u32[]{:S(2)}, u32[]{:S(2)}) collective-permute-start(bf16[2,128,1024]{2,1,0:T(8,128)(2,1)S(1)} %pad_maximum_fusion.41), channel_id=1, source_target_pairs={{0,4},{1,5},{2,6},{3,7},{4,0},{5,1},{6,2},{7,3},{8,12},{9,13},{10,... | collective-permute-start | bytes 1572872 | tf_op jit(solution)/shard_map/ppermute | solution.py:32
  230.3 254.1 %reduce-scatter.2.cloned.1.call-start = ((), (), s32[]{:S(2)}) async-start(), calls=%async_computation.3 | async-start | bytes 10485760 | tf_op jit(solution)/shard_map/reduce_scatter | solution.py:1033
  230.8 31.0 %collective-permute-start.32 = (bf16[16,128,1024]{2,1,0:T(8,128)(2,1)}, bf16[16,128,1024]{2,1,0:T(8,128)(2,1)}, u32[]{:S(2)}, u32[]{:S(2)}) collective-permute-start(bf16[16,128,1024]{2,1,0:T(8,128)(2,1)} %all-gather.3.cloned.1.call-done), channel_id=1, source_target_pairs={{0,1},{1,0},{2,3},{3,2},{4,5},{5,4},{6,7},{7,6},{8,9},{9,8},{10,11... | collective-permute-start | bytes 12582920 | tf_op jit(solution)/shard_map/ppermute | solution.py:32
  411.9 78.2 %collective-permute-start.55 = (bf16[208,1024]{1,0:T(8,128)(2,1)}, bf16[208,1024]{1,0:T(8,128)(2,1)S(1)}, u32[]{:S(2)}, u32[]{:S(2)}) collective-permute-start(bf16[208,1024]{1,0:T(8,128)(2,1)} %get-tuple-element.547), channel_id=1, source_target_pairs={{0,0},{4,1},{1,2},{5,3},{2,4},{6,5},{3,6},{7,7},{8,8},{12,9},{9,10... | collective-permute-start | bytes 1277960 | tf_op jit(solution)/shard_map/ppermute | solution.py:98
  413.6 76.5 %collective-permute-start.56 = (bf16[208,1024]{1,0:T(8,128)(2,1)}, bf16[208,1024]{1,0:T(8,128)(2,1)}, u32[]{:S(2)}, u32[]{:S(2)}) collective-permute-start(bf16[208,1024]{1,0:T(8,128)(2,1)} %get-tuple-element.546), channel_id=1, source_target_pairs={{4,0},{0,1},{5,2},{1,3},{6,4},{2,5},{7,6},{3,7},{12,8},{8,9},{13,1... | collective-permute-start | bytes 1277960 | tf_op jit(solution)/shard_map/ppermute | solution.py:106
  448.6 53.8 %collective-permute-start.59 = (bf16[2048,1024]{1,0:T(8,128)(2,1)}, bf16[2048,1024]{1,0:T(8,128)(2,1)}, u32[]{:S(2)}, u32[]{:S(2)}) collective-permute-start(bf16[2048,1024]{1,0:T(8,128)(2,1)} %pad_maximum_fusion), channel_id=1, source_target_pairs={{0,1},{1,0},{2,3},{3,2},{4,5},{5,4},{6,7},{7,6},{8,9},{9,8},{10,11... | collective-permute-start | bytes 12582920 | tf_op jit(solution)/shard_map/ppermute | solution.py:32
  495.9 31.4 %collective-permute-start.61 = (bf16[2,256,1024]{2,1,0:T(8,128)(2,1)}, bf16[2,256,1024]{2,1,0:T(8,128)(2,1)}, u32[]{:S(2)}, u32[]{:S(2)}) collective-permute-start(bf16[2,256,1024]{2,1,0:T(8,128)(2,1)} %slice.710), channel_id=1, source_target_pairs={{0,2},{1,3},{2,0},{3,1},{4,6},{5,7},{6,4},{7,5},{8,10},{9,11},{10,... | collective-permute-start | bytes 3145736 | tf_op jit(solution)/shard_map/ppermute | solution.py:32
  510.2 29.3 %collective-permute-start.60 = (bf16[416,1024]{1,0:T(8,128)(2,1)}, bf16[416,1024]{1,0:T(8,128)(2,1)}, u32[]{:S(2)}, u32[]{:S(2)}) collective-permute-start(bf16[416,1024]{1,0:T(8,128)(2,1)} %add_convert_fusion.5), channel_id=1, source_target_pairs={{0,2},{1,3},{2,0},{3,1},{4,6},{5,7},{6,4},{7,5},{8,10},{9,11},{10,... | collective-permute-start | bytes 2555912 | tf_op jit(solution)/shard_map/ppermute | solution.py:32
  555.0 34.5 %collective-permute-start.66 = (bf16[704,1024]{1,0:T(8,128)(2,1)S(1)}, bf16[704,1024]{1,0:T(8,128)(2,1)S(1)}, u32[]{:S(2)}, u32[]{:S(2)}) collective-permute-start(bf16[704,1024]{1,0:T(8,128)(2,1)S(1)} %pad_maximum_fusion.12), channel_id=1, source_target_pairs={{0,8},{8,0},{16,24},{24,16},{1,9},{9,1},{17,25},{25,17},{2,10},{10... | collective-permute-start | bytes 4325384 | tf_op jit(solution)/shard_map/ppermute | solution.py:32
  557.9 34.5 %collective-permute-start.67 = (bf16[704,1024]{1,0:T(8,128)(2,1)S(1)}, bf16[704,1024]{1,0:T(8,128)(2,1)S(1)}, u32[]{:S(2)}, u32[]{:S(2)}) collective-permute-start(bf16[704,1024]{1,0:T(8,128)(2,1)S(1)} %pad_maximum_fusion.13), channel_id=1, source_target_pairs={{0,16},{8,24},{16,0},{24,8},{1,17},{9,25},{17,1},{25,9},{2,18},{10... | collective-permute-start | bytes 4325384 | tf_op jit(solution)/shard_map/ppermute | solution.py:32
  572.8 29.7 %collective-permute-start.69 = (bf16[256,1024]{1,0:T(8,128)(2,1)S(1)}, bf16[256,1024]{1,0:T(8,128)(2,1)S(1)}, u32[]{:S(2)}, u32[]{:S(2)}) collective-permute-start(bf16[256,1024]{1,0:T(8,128)(2,1)S(1)} %get-tuple-element.466), channel_id=1, source_target_pairs={{0,16},{8,24},{16,0},{24,8},{1,17},{9,25},{17,1},{25,9},{2,18},{10... | collective-permute-start | bytes 1572872 | tf_op jit(solution)/shard_map/ppermute | solution.py:32
  604.8 29.1 %collective-permute-start.71 = (bf16[1024,1024]{1,0:T(8,128)(2,1)}, bf16[1024,1024]{1,0:T(8,128)(2,1)S(1)}, u32[]{:S(2)}, u32[]{:S(2)}) collective-permute-start(bf16[1024,1024]{1,0:T(8,128)(2,1)} %convolution_convert_fusion.8), channel_id=1, source_target_pairs={{0,1},{1,0},{2,3},{3,2},{4,5},{5,4},{6,7},{7,6},{8,9},{9,8},{10,11... | collective-permute-start | bytes 6291464 | tf_op jit(solution)/shard_map/ppermute | solution.py:32
  639.3 31.1 %collective-permute-start.76 = (bf16[256,1024]{1,0:T(8,128)(2,1)}, bf16[256,1024]{1,0:T(8,128)(2,1)}, u32[]{:S(2)}, u32[]{:S(2)}) collective-permute-start(bf16[256,1024]{1,0:T(8,128)(2,1)} %get-tuple-element.460), channel_id=1, source_target_pairs={{0,8},{8,0},{16,24},{24,16},{1,9},{9,1},{17,25},{25,17},{2,10},{10... | collective-permute-start | bytes 1572872 | tf_op jit(solution)/shard_map/ppermute | solution.py:32
  640.5 29.8 %collective-permute-start.77 = (bf16[256,1024]{1,0:T(8,128)(2,1)}, bf16[256,1024]{1,0:T(8,128)(2,1)}, u32[]{:S(2)}, u32[]{:S(2)}) collective-permute-start(bf16[256,1024]{1,0:T(8,128)(2,1)} %get-tuple-element.459), channel_id=1, source_target_pairs={{0,16},{8,24},{16,0},{24,8},{1,17},{9,25},{17,1},{25,9},{2,18},{10... | collective-permute-start | bytes 1572872 | tf_op jit(solution)/shard_map/ppermute | solution.py:32
  (277 other events, 2714.3 us)
Sparse Core Ops, SparseCore 0:
  160.7 50.3 all-gather.2
  230.4 87.3 all-gather.4
  395.4 85.5 reduce-scatter.1
